TPU v7x, 128 devices: a whole 4x4x4 slice. The times are simulated.
128 devices in a mesh: layer: 8 (over x_hi, y), query: 16 (over z, x_lo, core).
Axes of the slice: x: 4 (x_hi: 2, x_lo: 2; x = x_hi * 2 + x_lo), y: 4, z: 4, core: 2. Of those that a mesh axis runs over, the one named last changes fastest.
Arguments:
- train_grads: bfloat16 [256, 160, 4096], P('query', 'layer'), may hold values from -6 to 6
- query_pre: bfloat16 [1024, 160, 4096], P('query', 'layer'), may hold values from -0.0078125 to 0.0078125
- basis_in: bfloat16 [160, 64, 64], P('layer'), may hold values from -0.75 to 0.75
- basis_out: bfloat16 [160, 64, 64], P('layer'), may hold values from -0.75 to 0.75
Outputs:
- scores: float32 [256, 1024], P('layer', 'query')
All inputs are finite; a program needn't handle non-finite values.
Results may differ from a plain program's by a relative error of at most 0.004.
Values may be sent and summed in bfloat16 or wider, within the bound.
A program may use at most 192 MiB of HBM per device.

v0:
```python
import jax
import jax.numpy as jnp
from jax import lax
from jax.sharding import PartitionSpec as P


def from_behind(value, axis, steps):
    count = lax.axis_size(axis)
    pairs = [(source, (source + steps) % count) for source in range(count)]
    return lax.ppermute(value, axis, pairs)


def rotate_block(block, basis_in, basis_out):
    count = block.shape[0]
    modules = block.shape[1]
    width = basis_in.shape[1]
    matrices = block.reshape(count, modules, width, width)
    half_swapped = jnp.einsum(
        "mij,emoi->mjeo", basis_in, matrices, preferred_element_type=jnp.float32
    ).astype(jnp.bfloat16)
    rotated_swapped = jnp.einsum(
        "mjeo,mop->mjep", half_swapped, basis_out, preferred_element_type=jnp.float32
    ).astype(jnp.bfloat16)
    return jnp.transpose(rotated_swapped, (2, 0, 1, 3)).reshape(count, modules, width * width)


def score_block(rotated, query_pre):
    return jnp.einsum("emk,qmk->eq", rotated, query_pre, preferred_element_type=jnp.float32)


def shards(train_grads, query_pre, basis_in, basis_out):
    count = train_grads.shape[0]
    width = basis_in.shape[1]
    cycle_size = lax.axis_size("query")
    position = lax.axis_index("query")
    query_rows = query_pre.shape[0]
    modules = query_pre.shape[1]
    query_swapped = jnp.transpose(
        query_pre.reshape(query_rows, modules, width, width), (0, 1, 3, 2)
    ).reshape(query_rows, modules, width * width)
    own_block = rotate_block(train_grads, basis_in, basis_out)
    totals = jnp.zeros((count * cycle_size, query_rows), jnp.float32)
    first = score_block(own_block, query_swapped)
    totals = lax.dynamic_update_slice_in_dim(totals, first, position * count, 0)

    def cycle_step(step, carry):
        block, running = carry
        block = from_behind(block, "query", 1)
        source = (position - step) % cycle_size
        piece_scores = score_block(block, query_swapped)
        running = lax.dynamic_update_slice_in_dim(running, piece_scores, source * count, 0)
        return (block, running)

    unused, totals = lax.fori_loop(1, cycle_size, cycle_step, (own_block, totals))
    return lax.psum_scatter(totals, "layer", scatter_dimension=0, tiled=True)


def solution(mesh):
    placed = (
        P("query", "layer", None),
        P("query", "layer", None),
        P("layer", None, None),
        P("layer", None, None),
    )
    return jax.shard_map(
        shards, mesh=mesh, in_specs=placed, out_specs=P("layer", "query"), check_vma=False
    )
```

profile of v0, /device:TPU:1, one launch (start us, length us, event | category | flops | bytes accessed | tf_op | source)
XLA Modules:
  0.0 805.7 jit_solution(2189016235857603709)
XLA Ops:
  6.5 29.3 %reshape.14 = bf16[64,20,64,64]{3,2,0,1:T(8,128)(2,1)} reshape(bf16[64,20,4096]{2,0,1:T(8,128)(2,1)} %param.7) | data formatting | bytes 20971520 | tf_op jit(solution)/shard_map/reshape | solution.py:39
  35.9 28.2 %copy.5 = bf16[64,20,64,64]{2,3,0,1:T(8,128)(2,1)} copy(bf16[64,20,64,64]{3,2,0,1:T(8,128)(2,1)} %reshape.14) | data formatting | bytes 20971520 | tf_op jit(solution)/shard_map/reshape | solution.py:39
  64.0 28.2 %reshape.15 = bf16[64,20,4096]{2,0,1:T(8,128)(2,1)} reshape(bf16[64,20,64,64]{3,2,0,1:T(8,128)(2,1)} %bitcast.45) | data formatting | bytes 20971520 | tf_op jit(solution)/shard_map/reshape | solution.py:40
  92.2 6.6 reshape.12
  98.8 10.0 %convert_bitcast_fusion = bf16[16,20,64,64]{3,2,0,1:T(8,128)(2,1)} fusion(bf16[16,20,64,64]{3,2,0,1:T(8,128)(2,1)} %reshape.12, bf16[20,64,64]{2,1,0:T(8,128)(2,1)S(1)} %copy-done, bf16[20,64,64]{2,1,0:T(8,128)(2,1)S(1)} %copy-done.4), kind=kOutput, calls=%fused_computation.2 | convolution fusion | flops 338165760 | bytes 5570560 | tf_op jit(solution)/shard_map/mjeo,mop->mjep/dot_general | solution.py:21
  108.8 8.1 %reshape.13 = bf16[16,20,4096]{2,0,1:T(8,128)(2,1)} reshape(bf16[16,20,64,64]{3,2,0,1:T(8,128)(2,1)} %convert_bitcast_fusion) | data formatting | bytes 5242880 | tf_op jit(solution)/shard_map/reshape | solution.py:24
  116.9 7.6 fusion.7
  124.4 579.5 %while.17 = (s32[]{:T(128)}, bf16[16,20,4096]{2,0,1:T(8,128)(2,1)}, f32[256,64]{1,0:T(8,128)S(1)}, bf16[64,20,4096]{2,0,1:T(8,128)(2,1)}, s32[]{:T(128)}, /*inde...) while((s32[]{:T(128)}, bf16[16,20,4096]{2,0,1:T(8,128)(2,1)}, f32[256,64]{1,0:T(8,128)S(1)}, ...), condition=%wide.region_1.2_spmd, body=%wide.region_0.1_spmd.sunk | while | flops 167772176 | bytes 28844344 | solution.py:54
  127.1 28.9 %collective-permute-done = bf16[16,20,4096]{2,0,1:T(8,128)(2,1)S(1)} collective-permute-done((bf16[16,20,4096]{2,0,1:T(8,128)(2,1)}, bf16[16,20,4096]{2,0,1:T(8,128)(2,1)S(1)}, u32[]{:S(2)}, u32[]{:S(2)}) %collective-permute-start) | collective-permute-done | bytes 2621472 | tf_op jit(solution)/shard_map/while/body/eval_jaxpr/ppermute | solution.py:10
  165.4 28.9 %collective-permute-done = bf16[16,20,4096]{2,0,1:T(8,128)(2,1)S(1)} collective-permute-done((bf16[16,20,4096]{2,0,1:T(8,128)(2,1)}, bf16[16,20,4096]{2,0,1:T(8,128)(2,1)S(1)}, u32[]{:S(2)}, u32[]{:S(2)}) %collective-permute-start) | collective-permute-done | bytes 2621472 | tf_op jit(solution)/shard_map/while/body/eval_jaxpr/ppermute | solution.py:10
  203.7 28.9 %collective-permute-done = bf16[16,20,4096]{2,0,1:T(8,128)(2,1)S(1)} collective-permute-done((bf16[16,20,4096]{2,0,1:T(8,128)(2,1)}, bf16[16,20,4096]{2,0,1:T(8,128)(2,1)S(1)}, u32[]{:S(2)}, u32[]{:S(2)}) %collective-permute-start) | collective-permute-done | bytes 2621472 | tf_op jit(solution)/shard_map/while/body/eval_jaxpr/ppermute | solution.py:10
  242.0 28.9 %collective-permute-done = bf16[16,20,4096]{2,0,1:T(8,128)(2,1)S(1)} collective-permute-done((bf16[16,20,4096]{2,0,1:T(8,128)(2,1)}, bf16[16,20,4096]{2,0,1:T(8,128)(2,1)S(1)}, u32[]{:S(2)}, u32[]{:S(2)}) %collective-permute-start) | collective-permute-done | bytes 2621472 | tf_op jit(solution)/shard_map/while/body/eval_jaxpr/ppermute | solution.py:10
  280.3 28.9 %collective-permute-done = bf16[16,20,4096]{2,0,1:T(8,128)(2,1)S(1)} collective-permute-done((bf16[16,20,4096]{2,0,1:T(8,128)(2,1)}, bf16[16,20,4096]{2,0,1:T(8,128)(2,1)S(1)}, u32[]{:S(2)}, u32[]{:S(2)}) %collective-permute-start) | collective-permute-done | bytes 2621472 | tf_op jit(solution)/shard_map/while/body/eval_jaxpr/ppermute | solution.py:10
  318.6 28.9 %collective-permute-done = bf16[16,20,4096]{2,0,1:T(8,128)(2,1)S(1)} collective-permute-done((bf16[16,20,4096]{2,0,1:T(8,128)(2,1)}, bf16[16,20,4096]{2,0,1:T(8,128)(2,1)S(1)}, u32[]{:S(2)}, u32[]{:S(2)}) %collective-permute-start) | collective-permute-done | bytes 2621472 | tf_op jit(solution)/shard_map/while/body/eval_jaxpr/ppermute | solution.py:10
  356.9 28.9 %collective-permute-done = bf16[16,20,4096]{2,0,1:T(8,128)(2,1)S(1)} collective-permute-done((bf16[16,20,4096]{2,0,1:T(8,128)(2,1)}, bf16[16,20,4096]{2,0,1:T(8,128)(2,1)S(1)}, u32[]{:S(2)}, u32[]{:S(2)}) %collective-permute-start) | collective-permute-done | bytes 2621472 | tf_op jit(solution)/shard_map/while/body/eval_jaxpr/ppermute | solution.py:10
  395.2 28.9 %collective-permute-done = bf16[16,20,4096]{2,0,1:T(8,128)(2,1)S(1)} collective-permute-done((bf16[16,20,4096]{2,0,1:T(8,128)(2,1)}, bf16[16,20,4096]{2,0,1:T(8,128)(2,1)S(1)}, u32[]{:S(2)}, u32[]{:S(2)}) %collective-permute-start) | collective-permute-done | bytes 2621472 | tf_op jit(solution)/shard_map/while/body/eval_jaxpr/ppermute | solution.py:10
  433.5 28.9 %collective-permute-done = bf16[16,20,4096]{2,0,1:T(8,128)(2,1)S(1)} collective-permute-done((bf16[16,20,4096]{2,0,1:T(8,128)(2,1)}, bf16[16,20,4096]{2,0,1:T(8,128)(2,1)S(1)}, u32[]{:S(2)}, u32[]{:S(2)}) %collective-permute-start) | collective-permute-done | bytes 2621472 | tf_op jit(solution)/shard_map/while/body/eval_jaxpr/ppermute | solution.py:10
  471.8 28.9 %collective-permute-done = bf16[16,20,4096]{2,0,1:T(8,128)(2,1)S(1)} collective-permute-done((bf16[16,20,4096]{2,0,1:T(8,128)(2,1)}, bf16[16,20,4096]{2,0,1:T(8,128)(2,1)S(1)}, u32[]{:S(2)}, u32[]{:S(2)}) %collective-permute-start) | collective-permute-done | bytes 2621472 | tf_op jit(solution)/shard_map/while/body/eval_jaxpr/ppermute | solution.py:10
  510.1 28.9 %collective-permute-done = bf16[16,20,4096]{2,0,1:T(8,128)(2,1)S(1)} collective-permute-done((bf16[16,20,4096]{2,0,1:T(8,128)(2,1)}, bf16[16,20,4096]{2,0,1:T(8,128)(2,1)S(1)}, u32[]{:S(2)}, u32[]{:S(2)}) %collective-permute-start) | collective-permute-done | bytes 2621472 | tf_op jit(solution)/shard_map/while/body/eval_jaxpr/ppermute | solution.py:10
  548.4 28.9 %collective-permute-done = bf16[16,20,4096]{2,0,1:T(8,128)(2,1)S(1)} collective-permute-done((bf16[16,20,4096]{2,0,1:T(8,128)(2,1)}, bf16[16,20,4096]{2,0,1:T(8,128)(2,1)S(1)}, u32[]{:S(2)}, u32[]{:S(2)}) %collective-permute-start) | collective-permute-done | bytes 2621472 | tf_op jit(solution)/shard_map/while/body/eval_jaxpr/ppermute | solution.py:10
  586.7 29.4 %collective-permute-done = bf16[16,20,4096]{2,0,1:T(8,128)(2,1)S(1)} collective-permute-done((bf16[16,20,4096]{2,0,1:T(8,128)(2,1)}, bf16[16,20,4096]{2,0,1:T(8,128)(2,1)S(1)}, u32[]{:S(2)}, u32[]{:S(2)}) %collective-permute-start) | collective-permute-done | bytes 2621472 | tf_op jit(solution)/shard_map/while/body/eval_jaxpr/ppermute | solution.py:10
  625.0 31.5 %collective-permute-done = bf16[16,20,4096]{2,0,1:T(8,128)(2,1)S(1)} collective-permute-done((bf16[16,20,4096]{2,0,1:T(8,128)(2,1)}, bf16[16,20,4096]{2,0,1:T(8,128)(2,1)S(1)}, u32[]{:S(2)}, u32[]{:S(2)}) %collective-permute-start) | collective-permute-done | bytes 2621472 | tf_op jit(solution)/shard_map/while/body/eval_jaxpr/ppermute | solution.py:10
  663.5 33.4 %collective-permute-done = bf16[16,20,4096]{2,0,1:T(8,128)(2,1)S(1)} collective-permute-done((bf16[16,20,4096]{2,0,1:T(8,128)(2,1)}, bf16[16,20,4096]{2,0,1:T(8,128)(2,1)S(1)}, u32[]{:S(2)}, u32[]{:S(2)}) %collective-permute-start) | collective-permute-done | bytes 2621472 | tf_op jit(solution)/shard_map/while/body/eval_jaxpr/ppermute | solution.py:10
  704.6 94.2 %reduce-scatter.2.cloned.1.call-done = f32[32,64]{1,0:T(8,128)} async-done(((f32[256,64]{1,0:T(8,128)}), f32[32,64]{1,0:T(8,128)}) %reduce-scatter.2.cloned.1.call-update) | async-done | bytes 8208 | tf_op jit(solution)/shard_map/reduce_scatter | solution.py:55
  (58 shorter events, 138.9 us)
Async XLA Ops:
  6.5 92.3 %copy-start = (bf16[20,64,64]{2,1,0:T(8,128)(2,1)S(1)}, bf16[20,64,64]{2,1,0:T(8,128)(2,1)}, u32[]{:S(2)}) copy-start(bf16[20,64,64]{2,1,0:T(8,128)(2,1)} %param.9) | copy-start | bytes 491524
  6.5 792.3 %reduce-scatter.2.cloned.1.call-start = ((), (), s32[]{:S(2)}) async-start(), calls=%async_computation.1 | async-start | bytes 147456 | tf_op jit(solution)/shard_map/reduce_scatter | solution.py:55
  64.0 28.2 %copy-start.2 = (bf16[16,20,4096]{2,0,1:T(8,128)(2,1)S(1)}, bf16[16,20,4096]{2,0,1:T(8,128)(2,1)}, u32[]{:S(2)}) copy-start(bf16[16,20,4096]{2,0,1:T(8,128)(2,1)} %param.6) | copy-start | bytes 7864324
  92.2 6.6 copy-start.4
  124.4 31.5 %collective-permute-start = (bf16[16,20,4096]{2,0,1:T(8,128)(2,1)}, bf16[16,20,4096]{2,0,1:T(8,128)(2,1)S(1)}, u32[]{:S(2)}, u32[]{:S(2)}) collective-permute-start(bf16[16,20,4096]{2,0,1:T(8,128)(2,1)} %get-tuple-element.191), channel_id=1, source_target_pairs={{0,1},{1,2},{2,3},{3,4},{4,5},{5,6},{6,7},{7,8},{8,9},{9,10},{10,1... | collective-permute-start | bytes 7864328 | tf_op jit(solution)/shard_map/while/body/eval_jaxpr/ppermute | solution.py:10
  163.0 31.3 %collective-permute-start = (bf16[16,20,4096]{2,0,1:T(8,128)(2,1)}, bf16[16,20,4096]{2,0,1:T(8,128)(2,1)S(1)}, u32[]{:S(2)}, u32[]{:S(2)}) collective-permute-start(bf16[16,20,4096]{2,0,1:T(8,128)(2,1)} %get-tuple-element.191), channel_id=1, source_target_pairs={{0,1},{1,2},{2,3},{3,4},{4,5},{5,6},{6,7},{7,8},{8,9},{9,10},{10,1... | collective-permute-start | bytes 7864328 | tf_op jit(solution)/shard_map/while/body/eval_jaxpr/ppermute | solution.py:10
  201.3 31.3 %collective-permute-start = (bf16[16,20,4096]{2,0,1:T(8,128)(2,1)}, bf16[16,20,4096]{2,0,1:T(8,128)(2,1)S(1)}, u32[]{:S(2)}, u32[]{:S(2)}) collective-permute-start(bf16[16,20,4096]{2,0,1:T(8,128)(2,1)} %get-tuple-element.191), channel_id=1, source_target_pairs={{0,1},{1,2},{2,3},{3,4},{4,5},{5,6},{6,7},{7,8},{8,9},{9,10},{10,1... | collective-permute-start | bytes 7864328 | tf_op jit(solution)/shard_map/while/body/eval_jaxpr/ppermute | solution.py:10
  239.6 31.3 %collective-permute-start = (bf16[16,20,4096]{2,0,1:T(8,128)(2,1)}, bf16[16,20,4096]{2,0,1:T(8,128)(2,1)S(1)}, u32[]{:S(2)}, u32[]{:S(2)}) collective-permute-start(bf16[16,20,4096]{2,0,1:T(8,128)(2,1)} %get-tuple-element.191), channel_id=1, source_target_pairs={{0,1},{1,2},{2,3},{3,4},{4,5},{5,6},{6,7},{7,8},{8,9},{9,10},{10,1... | collective-permute-start | bytes 7864328 | tf_op jit(solution)/shard_map/while/body/eval_jaxpr/ppermute | solution.py:10
  277.9 31.3 %collective-permute-start = (bf16[16,20,4096]{2,0,1:T(8,128)(2,1)}, bf16[16,20,4096]{2,0,1:T(8,128)(2,1)S(1)}, u32[]{:S(2)}, u32[]{:S(2)}) collective-permute-start(bf16[16,20,4096]{2,0,1:T(8,128)(2,1)} %get-tuple-element.191), channel_id=1, source_target_pairs={{0,1},{1,2},{2,3},{3,4},{4,5},{5,6},{6,7},{7,8},{8,9},{9,10},{10,1... | collective-permute-start | bytes 7864328 | tf_op jit(solution)/shard_map/while/body/eval_jaxpr/ppermute | solution.py:10
  316.2 31.3 %collective-permute-start = (bf16[16,20,4096]{2,0,1:T(8,128)(2,1)}, bf16[16,20,4096]{2,0,1:T(8,128)(2,1)S(1)}, u32[]{:S(2)}, u32[]{:S(2)}) collective-permute-start(bf16[16,20,4096]{2,0,1:T(8,128)(2,1)} %get-tuple-element.191), channel_id=1, source_target_pairs={{0,1},{1,2},{2,3},{3,4},{4,5},{5,6},{6,7},{7,8},{8,9},{9,10},{10,1... | collective-permute-start | bytes 7864328 | tf_op jit(solution)/shard_map/while/body/eval_jaxpr/ppermute | solution.py:10
  354.5 31.3 %collective-permute-start = (bf16[16,20,4096]{2,0,1:T(8,128)(2,1)}, bf16[16,20,4096]{2,0,1:T(8,128)(2,1)S(1)}, u32[]{:S(2)}, u32[]{:S(2)}) collective-permute-start(bf16[16,20,4096]{2,0,1:T(8,128)(2,1)} %get-tuple-element.191), channel_id=1, source_target_pairs={{0,1},{1,2},{2,3},{3,4},{4,5},{5,6},{6,7},{7,8},{8,9},{9,10},{10,1... | collective-permute-start | bytes 7864328 | tf_op jit(solution)/shard_map/while/body/eval_jaxpr/ppermute | solution.py:10
  392.8 31.3 %collective-permute-start = (bf16[16,20,4096]{2,0,1:T(8,128)(2,1)}, bf16[16,20,4096]{2,0,1:T(8,128)(2,1)S(1)}, u32[]{:S(2)}, u32[]{:S(2)}) collective-permute-start(bf16[16,20,4096]{2,0,1:T(8,128)(2,1)} %get-tuple-element.191), channel_id=1, source_target_pairs={{0,1},{1,2},{2,3},{3,4},{4,5},{5,6},{6,7},{7,8},{8,9},{9,10},{10,1... | collective-permute-start | bytes 7864328 | tf_op jit(solution)/shard_map/while/body/eval_jaxpr/ppermute | solution.py:10
  431.1 31.3 %collective-permute-start = (bf16[16,20,4096]{2,0,1:T(8,128)(2,1)}, bf16[16,20,4096]{2,0,1:T(8,128)(2,1)S(1)}, u32[]{:S(2)}, u32[]{:S(2)}) collective-permute-start(bf16[16,20,4096]{2,0,1:T(8,128)(2,1)} %get-tuple-element.191), channel_id=1, source_target_pairs={{0,1},{1,2},{2,3},{3,4},{4,5},{5,6},{6,7},{7,8},{8,9},{9,10},{10,1... | collective-permute-start | bytes 7864328 | tf_op jit(solution)/shard_map/while/body/eval_jaxpr/ppermute | solution.py:10
  469.4 31.3 %collective-permute-start = (bf16[16,20,4096]{2,0,1:T(8,128)(2,1)}, bf16[16,20,4096]{2,0,1:T(8,128)(2,1)S(1)}, u32[]{:S(2)}, u32[]{:S(2)}) collective-permute-start(bf16[16,20,4096]{2,0,1:T(8,128)(2,1)} %get-tuple-element.191), channel_id=1, source_target_pairs={{0,1},{1,2},{2,3},{3,4},{4,5},{5,6},{6,7},{7,8},{8,9},{9,10},{10,1... | collective-permute-start | bytes 7864328 | tf_op jit(solution)/shard_map/while/body/eval_jaxpr/ppermute | solution.py:10
  507.7 31.3 %collective-permute-start = (bf16[16,20,4096]{2,0,1:T(8,128)(2,1)}, bf16[16,20,4096]{2,0,1:T(8,128)(2,1)S(1)}, u32[]{:S(2)}, u32[]{:S(2)}) collective-permute-start(bf16[16,20,4096]{2,0,1:T(8,128)(2,1)} %get-tuple-element.191), channel_id=1, source_target_pairs={{0,1},{1,2},{2,3},{3,4},{4,5},{5,6},{6,7},{7,8},{8,9},{9,10},{10,1... | collective-permute-start | bytes 7864328 | tf_op jit(solution)/shard_map/while/body/eval_jaxpr/ppermute | solution.py:10
  546.0 31.3 %collective-permute-start = (bf16[16,20,4096]{2,0,1:T(8,128)(2,1)}, bf16[16,20,4096]{2,0,1:T(8,128)(2,1)S(1)}, u32[]{:S(2)}, u32[]{:S(2)}) collective-permute-start(bf16[16,20,4096]{2,0,1:T(8,128)(2,1)} %get-tuple-element.191), channel_id=1, source_target_pairs={{0,1},{1,2},{2,3},{3,4},{4,5},{5,6},{6,7},{7,8},{8,9},{9,10},{10,1... | collective-permute-start | bytes 7864328 | tf_op jit(solution)/shard_map/while/body/eval_jaxpr/ppermute | solution.py:10
  584.3 31.8 %collective-permute-start = (bf16[16,20,4096]{2,0,1:T(8,128)(2,1)}, bf16[16,20,4096]{2,0,1:T(8,128)(2,1)S(1)}, u32[]{:S(2)}, u32[]{:S(2)}) collective-permute-start(bf16[16,20,4096]{2,0,1:T(8,128)(2,1)} %get-tuple-element.191), channel_id=1, source_target_pairs={{0,1},{1,2},{2,3},{3,4},{4,5},{5,6},{6,7},{7,8},{8,9},{9,10},{10,1... | collective-permute-start | bytes 7864328 | tf_op jit(solution)/shard_map/while/body/eval_jaxpr/ppermute | solution.py:10
  623.1 33.4 %collective-permute-start = (bf16[16,20,4096]{2,0,1:T(8,128)(2,1)}, bf16[16,20,4096]{2,0,1:T(8,128)(2,1)S(1)}, u32[]{:S(2)}, u32[]{:S(2)}) collective-permute-start(bf16[16,20,4096]{2,0,1:T(8,128)(2,1)} %get-tuple-element.191), channel_id=1, source_target_pairs={{0,1},{1,2},{2,3},{3,4},{4,5},{5,6},{6,7},{7,8},{8,9},{9,10},{10,1... | collective-permute-start | bytes 7864328 | tf_op jit(solution)/shard_map/while/body/eval_jaxpr/ppermute | solution.py:10
  663.5 33.4 %collective-permute-start = (bf16[16,20,4096]{2,0,1:T(8,128)(2,1)}, bf16[16,20,4096]{2,0,1:T(8,128)(2,1)S(1)}, u32[]{:S(2)}, u32[]{:S(2)}) collective-permute-start(bf16[16,20,4096]{2,0,1:T(8,128)(2,1)} %get-tuple-element.191), channel_id=1, source_target_pairs={{0,1},{1,2},{2,3},{3,4},{4,5},{5,6},{6,7},{7,8},{8,9},{9,10},{10,1... | collective-permute-start | bytes 7864328 | tf_op jit(solution)/shard_map/while/body/eval_jaxpr/ppermute | solution.py:10
  703.9 0.7 copy-start.3
  703.9 94.9 %copy-start.1 = (bf16[20,64,64]{2,1,0:T(8,128)(2,1)S(1)}, bf16[20,64,64]{2,1,0:T(8,128)(2,1)}, u32[]{:S(2)}) copy-start(bf16[20,64,64]{2,1,0:T(8,128)(2,1)} %param.9) | copy-start | bytes 491524
Sparse Core Ops, SparseCore 0:
  704.7 94.0 reduce-scatter.1
where the time goes:
time: 809 us; the launch traced here: 806 us
  waiting for transfers between devices  535 us (66%)
  local copies, waits for them, and re-layouts  123 us (15%)
  matrix products  100 us (12%)
  starting transfers between devices  33.2 us (4%)
  between operations  13.4 us (2%)
    ppermute x15, waiting for transfers between devices, from_behind(): return lax.ppermute(value, axis, pairs)  441 us
    reduce_scatter x1, waiting for transfers between devices, shards(): return lax.psum_scatter(totals, 'layer', scatter_dimension=0, tiled=True)  94.2 us
    dot_general x16, matrix products, score_block(): jnp.einsum('emk,qmk->eq', rotated, query_pre, preferred_element_type=jnp....  90.3 us
    reshape x2, local copies, waits for them, and re-layouts, shards(): query_pre.reshape(query_rows, modules, width, width)  57.5 us
    ppermute x15, starting transfers between devices, from_behind(): return lax.ppermute(value, axis, pairs)  33.2 us
    reshape x1, local copies, waits for them, and re-layouts, shards(): query_swapped = jnp.transpose(query_pre.reshape(query_rows, modules, widt...  28.2 us
    while x15, local copies, waits for them, and re-layouts  22.3 us
  transfers between devices with their start and end apart: 16, of which 16 were waited for; matrix products, arithmetic and copies ran while one was open for 0% of the time, Pallas kernels for 0%

commit v1 on v0

v1 whole, which is shorter than its diff:
```python
import jax
import jax.numpy as jnp
from jax import lax
from jax.experimental import pallas as pl
from jax.experimental.pallas import tpu as pltpu
from jax.sharding import PartitionSpec as P

MESH = pl.DeviceIdType.MESH
BF16 = jnp.bfloat16
F32 = jnp.float32

WIDTH = 64
FLAT = WIDTH * WIDTH
MODULES = 20
OWN_TRAIN = 16
OWN_QUERY = 64
LAYERS = 8
DEPTH = 4
PAIR_SLOTS = 3
COLUMN_SLOTS = 4
SLOTS = PAIR_SLOTS + COLUMN_SLOTS
LANES = 128
CHUNKS = FLAT // LANES
PARTNERS = ((0, 1), (1, 0), (1, 1))


def dot(a, b):
    return jnp.dot(a, b, preferred_element_type=F32)


def dot_t(a, b):
    return lax.dot_general(a, b, (((1,), (1,)), ((), ())), preferred_element_type=F32)


def iota(shape, dim):
    return lax.broadcasted_iota(jnp.int32, shape, dim)


def one_hot(condition):
    return jnp.where(condition, 1.0, 0.0).astype(BF16)


def kernel(
    train_hbm, query_hbm, inner_ref, outer_ref, out_ref,
    train, query, padded, padded_query, swapped, rotated, queries, blocks, pair_queries, column_queries,
    swap, spread_rows, spread_lanes, keep, columns_of, rows_even, rows_odd,
    pair_scores, column_scores, mine, theirs, gathered, total, sib_total,
    train_sem, query_sem, local_sem, local_query_sem,
    block_send, block_recv, ring_send, ring_recv, half_send, half_recv,
    query_send, query_recv, pair_send, pair_recv, layer_send, layer_recv, core_send, core_recv,
):
    layer = lax.axis_index("layer")
    place = lax.axis_index("query")
    z = place // 4
    column = (place // 2) % 2
    core = place % 2
    here = place % 4

    def at_plane(other_column, other_core):
        x = 1 - column if other_column else column
        c = 1 - core if other_core else core
        return x, c, (layer, z * 4 + x * 2 + c)

    def at_ring(step):
        return (layer, ((z + step + DEPTH) % DEPTH) * 4 + here)

    load_train = pltpu.make_async_copy(train_hbm, train, train_sem)
    load_train.start()

    def load_query(part):
        return pltpu.make_async_copy(
            query_hbm.at[pl.ds(part * 16, 16)], query.at[part % 2], query_sem.at[part % 2]
        )

    load_query(0).start()
    load_query(1).start()

    barrier = pltpu.get_barrier_semaphore()
    for partner in PARTNERS:
        pl.semaphore_signal(barrier, inc=1, device_id=at_plane(*partner)[2], device_id_type=MESH)
    for step in (1, -1):
        pl.semaphore_signal(barrier, inc=1, device_id=at_ring(step), device_id_type=MESH)
    for step in range(1, LAYERS):
        pl.semaphore_signal(
            barrier, inc=1, device_id=((layer + step) % LAYERS, place), device_id_type=MESH
        )

    row, col = iota((256, 256), 0), iota((256, 256), 1)
    swap[...] = one_hot((row // 16 == col % 16) & (row % 16 == col // 16))
    row, col = iota((128, 64), 0), iota((128, 64), 1)
    spread_rows[...] = one_hot(row % 64 == col)
    row, col = iota((64, 256), 0), iota((64, 256), 1)
    spread_lanes[...] = one_hot(col % 64 == row)
    row, col = iota((128, 256), 0), iota((128, 256), 1)
    group = col // 64
    keep[...] = jnp.where(((group == 0) | (group == 3)) == (row < 64), 1.0, 0.0)
    row, col = iota((64, 64), 0), iota((64, 64), 1)
    columns_of[...] = one_hot(col == 2 * (row % 32) + row // 32)
    rows_even[...] = one_hot(row == 2 * (col % 32) + col // 32)
    rows_odd[...] = one_hot(row == 2 * (col % 32) + 1 - col // 32)
    padded[...] = jnp.zeros_like(padded)
    padded_query[...] = jnp.zeros_like(padded_query)

    pl.semaphore_wait(barrier, len(PARTNERS) + 2 + LAYERS - 1)

    def store_swapped(first, count, example, value):
        pieces = jnp.concatenate(
            [
                jnp.concatenate(
                    [value[:, (16 * half + c) * LANES:(16 * half + c + 1) * LANES] for c in range(16)], axis=0
                )
                for half in range(2)
            ],
            axis=1,
        )
        turned = dot(swap[0:16 * count, :], pieces).astype(BF16)
        for m in range(count):
            for half in range(2):
                swapped[first + m, example, 16 * half:16 * half + 16, :] = turned[
                    16 * m:16 * m + 16, half * LANES:(half + 1) * LANES
                ]

    def turn_train(example, carry):
        store_swapped(0, 16, example, train[example, 0:16, :])
        return carry

    def turn_train_rest(example, carry):
        padded[0:4, :] = train[example, 16:20, :]
        store_swapped(16, 4, example, padded[...])
        return carry

    def rotate(m, carry):
        inner = dot(dot(spread_rows[...], inner_ref[m]).astype(BF16), spread_lanes[...])
        inner = (inner * keep[...]).astype(BF16)
        turned = dot_t(columns_of[...], outer_ref[m]).astype(BF16)
        outer = jnp.where(
            iota((64, 64), 0) < 32, dot(turned, rows_even[...]), dot(turned, rows_odd[...])
        ).astype(BF16)
        half = dot(swapped[m].reshape(512, LANES), inner).astype(BF16)
        stacked = jnp.concatenate(
            [
                jnp.concatenate(
                    [half[32 * e:32 * e + 32, h * LANES:(h + 1) * LANES] for e in range(OWN_TRAIN)], axis=1
                )
                for h in range(2)
            ],
            axis=0,
        )
        both = dot(outer, stacked)
        first = iota((32, OWN_TRAIN * LANES), 1) % LANES < WIDTH
        result = jnp.where(first, both[:32], both[32:]).astype(BF16)
        pieces = jnp.concatenate(
            [
                jnp.concatenate(
                    [result[16 * h:16 * h + 16, e * LANES:(e + 1) * LANES] for e in range(OWN_TRAIN)], axis=0
                )
                for h in range(2)
            ],
            axis=1,
        )
        final = dot(swap[...], pieces).astype(BF16)
        rotated[m] = jnp.concatenate(
            [final[16 * c:16 * c + 16, h * LANES:(h + 1) * LANES] for h in range(2) for c in range(16)], axis=1
        )
        return carry

    def turn_query(part):
        load_query(part).wait()
        slot = part % 2
        rows = pl.ds(pl.multiple_of(part * 16, 16), 16)

        def lanes_step(step, carry):
            lanes = pl.ds(pl.multiple_of(step * 256, 256), 256)
            turned = dot(swap[...], query[slot, :, 0:16, lanes].reshape(256, 256)).astype(BF16)
            for m in range(16):
                queries[m, rows, lanes] = turned[16 * m:16 * m + 16]
            for q in range(16):
                padded_query[q, 0:4, :] = query[slot, q, 16:20, lanes]
            turned = dot(swap[0:64, :], padded_query[...].reshape(256, 256)).astype(BF16)
            for m in range(4):
                queries[16 + m, rows, lanes] = turned[16 * m:16 * m + 16]
            return carry

        lax.fori_loop(0, FLAT // 256, lanes_step, 0)

    def block_copy(slot, partner):
        x, c, device = at_plane(*PARTNERS[partner])
        m = 4 * slot + 2 * x + c if slot < PAIR_SLOTS else 6 + 2 * slot + c
        return pltpu.make_async_remote_copy(
            src_ref=rotated.at[m],
            dst_ref=blocks.at[slot, z, pl.ds(pl.multiple_of(here * 16, 16), 16)],
            send_sem=block_send.at[slot, partner],
            recv_sem=block_recv.at[slot, partner],
            device_id=device,
            device_id_type=MESH,
        )

    def own_copy(slot):
        m = 4 * slot + here if slot < PAIR_SLOTS else 6 + 2 * slot + core
        return pltpu.make_async_copy(
            rotated.at[m], blocks.at[slot, z, pl.ds(pl.multiple_of(here * 16, 16), 16)], local_sem.at[slot]
        )

    def ring_copy(slot, way):
        return pltpu.make_async_remote_copy(
            src_ref=blocks.at[slot, z],
            dst_ref=blocks.at[slot, z],
            send_sem=ring_send.at[slot, way],
            recv_sem=ring_recv.at[slot, way],
            device_id=at_ring(1 - 2 * way),
            device_id_type=MESH,
        )

    def half_copy(slot, way):
        source = (z + DEPTH - 1 + 2 * way) % DEPTH
        half = blocks.at[slot, source, pl.ds(32 * way, 32)]
        return pltpu.make_async_remote_copy(
            src_ref=half,
            dst_ref=half,
            send_sem=half_send.at[slot, way],
            recv_sem=half_recv.at[slot, way],
            device_id=at_ring(1 - 2 * way),
            device_id_type=MESH,
        )

    def query_copy(slot, partner, part=None):
        x, c, device = at_plane(*PARTNERS[partner])
        rows = pl.ds(0, 64) if part is None else pl.ds(16 * part, 16)
        to = pl.ds(pl.multiple_of(core * 64, 64) if part is None else pl.multiple_of(core * 64 + part * 16, 16), 64 if part is None else 16)
        if slot < PAIR_SLOTS:
            m, target = 4 * slot + 2 * x + c, pair_queries.at[slot, PARTNERS[partner][0], to]
        else:
            m, target = 6 + 2 * slot + c, column_queries.at[slot - PAIR_SLOTS, to]
        return pltpu.make_async_remote_copy(
            src_ref=queries.at[m, rows],
            dst_ref=target,
            send_sem=query_send.at[slot, partner],
            recv_sem=query_recv.at[slot, partner],
            device_id=device,
            device_id_type=MESH,
        )

    def own_query_copy(slot):
        to = pl.ds(pl.multiple_of(core * 64, 64), 64)
        if slot < PAIR_SLOTS:
            m, target = 4 * slot + here, pair_queries.at[slot, 0, to]
        else:
            m, target = 6 + 2 * slot + core, column_queries.at[slot - PAIR_SLOTS, to]
        return pltpu.make_async_copy(queries.at[m], target, local_query_sem.at[slot])

    def send_blocks(slot):
        for partner in (1, 2, 0):
            block_copy(slot, partner).start()
        own_copy(slot).start()

    def send_ring(slot):
        for partner in range(3):
            block_copy(slot, partner).wait_recv()
        own_copy(slot).wait()
        for way in range(2):
            ring_copy(slot, way).start()

    def send_half(slot):
        for way in range(2):
            ring_copy(slot, way).wait_recv()
            half_copy(slot, way).start()

    def query_partners(slot):
        return (1, 2, 0) if slot < PAIR_SLOTS else (0,)

    def send_queries(part):
        for slot in range(PAIR_SLOTS):
            for partner in query_partners(slot):
                query_copy(slot, partner, part).start()

    load_train.wait()
    lax.fori_loop(0, OWN_TRAIN, turn_train, 0)
    lax.fori_loop(0, 4, rotate, 0)
    send_blocks(0)
    lax.fori_loop(4, 8, rotate, 0)
    send_blocks(1)
    send_ring(0)
    turn_query(0)
    load_query(2).start()
    send_queries(0)
    lax.fori_loop(8, 12, rotate, 0)
    send_blocks(2)
    send_ring(1)
    turn_query(1)
    load_query(3).start()
    send_queries(1)
    lax.fori_loop(0, OWN_TRAIN, turn_train_rest, 0)
    lax.fori_loop(12, 16, rotate, 0)
    send_blocks(3)
    send_blocks(4)
    send_ring(2)
    turn_query(2)
    send_queries(2)
    send_ring(3)
    lax.fori_loop(16, 20, rotate, 0)
    send_blocks(5)
    send_blocks(6)
    send_ring(4)
    turn_query(3)
    send_queries(3)
    for slot in range(PAIR_SLOTS, SLOTS):
        query_copy(slot, 0).start()
    for slot in range(SLOTS):
        own_query_copy(slot).start()
    send_ring(5)
    send_ring(6)
    for slot in range(SLOTS):
        send_half(slot)

    def wait_blocks(slot):
        for way in range(2):
            half_copy(slot, way).wait_recv()
        for partner in query_partners(slot):
            query_copy(slot, partner).wait_recv()
        own_query_copy(slot).wait()

    pair_scores[...] = jnp.zeros_like(pair_scores)
    column_scores[...] = jnp.zeros_like(column_scores)
    for slot in range(PAIR_SLOTS):
        wait_blocks(slot)

        def pair_step(step, carry):
            lanes = pl.ds(pl.multiple_of(step * 512, 512), 512)
            rows = blocks[slot, :, :, lanes].reshape(256, 512)
            for side in range(2):
                pair_scores[side] += dot_t(rows, pair_queries[slot, side, :, lanes])
            return carry

        lax.fori_loop(0, FLAT // 512, pair_step, 0)

    cross = pltpu.make_async_remote_copy(
        src_ref=pair_scores.at[1],
        dst_ref=theirs,
        send_sem=pair_send,
        recv_sem=pair_recv,
        device_id=at_plane(1, 0)[2],
        device_id_type=MESH,
    )
    cross.start()
    for slot in range(PAIR_SLOTS, SLOTS):
        wait_blocks(slot)

        def column_step(step, carry):
            lanes = pl.ds(pl.multiple_of(step * 512, 512), 512)
            rows = blocks[slot, :, :, lanes].reshape(256, 512)
            column_scores[...] += dot_t(rows, column_queries[slot - PAIR_SLOTS, :, lanes])
            return carry

        lax.fori_loop(0, FLAT // 512, column_step, 0)
    cross.wait_recv()
    mine[...] = (pair_scores[0] + column_scores[...] + theirs[...]).reshape(LAYERS, 32, LANES)

    def layer_copy(step):
        return pltpu.make_async_remote_copy(
            src_ref=mine.at[(layer + step) % LAYERS],
            dst_ref=gathered.at[step],
            send_sem=layer_send.at[step],
            recv_sem=layer_recv.at[step],
            device_id=((layer + step) % LAYERS, place),
            device_id_type=MESH,
        )

    for step in range(1, LAYERS):
        layer_copy(step).start()
    total[...] = mine[layer]
    for step in range(1, LAYERS):
        layer_copy(step).wait_recv()
        total[...] += gathered[step]
    between = pltpu.make_async_remote_copy(
        src_ref=total,
        dst_ref=sib_total,
        send_sem=core_send,
        recv_sem=core_recv,
        device_id=at_plane(0, 1)[2],
        device_id_type=MESH,
    )
    between.start()
    between.wait()
    both = total[...] + sib_total[...]
    out_ref[...] = jnp.where(core == 0, both[:, :WIDTH], both[:, WIDTH:])

    for step in range(1, LAYERS):
        layer_copy(step).wait_send()
    cross.wait_send()
    for slot in range(SLOTS):
        for partner in range(3):
            block_copy(slot, partner).wait_send()
        for partner in query_partners(slot):
            query_copy(slot, partner).wait_send()
        for way in range(2):
            ring_copy(slot, way).wait_send()
            half_copy(slot, way).wait_send()


def shards(train_grads, query_pre, basis_in, basis_out):
    dma = pltpu.SemaphoreType.DMA
    return pl.pallas_call(
        kernel,
        out_shape=jax.ShapeDtypeStruct((32, WIDTH), F32),
        in_specs=[
            pl.BlockSpec(memory_space=pl.ANY),
            pl.BlockSpec(memory_space=pl.ANY),
            pl.BlockSpec(memory_space=pltpu.VMEM),
            pl.BlockSpec(memory_space=pltpu.VMEM),
        ],
        out_specs=pl.BlockSpec(memory_space=pltpu.VMEM),
        scratch_shapes=[
            pltpu.VMEM((OWN_TRAIN, MODULES, FLAT), BF16),
            pltpu.VMEM((2, 16, MODULES, FLAT), BF16),
            pltpu.VMEM((16, FLAT), BF16),
            pltpu.VMEM((16, 16, 256), BF16),
            pltpu.VMEM((MODULES, OWN_TRAIN, CHUNKS, LANES), BF16),
            pltpu.VMEM((MODULES, OWN_TRAIN, FLAT), BF16),
            pltpu.VMEM((MODULES, OWN_QUERY, FLAT), BF16),
            pltpu.VMEM((SLOTS, DEPTH, 64, FLAT), BF16),
            pltpu.VMEM((PAIR_SLOTS, 2, 128, FLAT), BF16),
            pltpu.VMEM((COLUMN_SLOTS, 128, FLAT), BF16),
            pltpu.VMEM((256, 256), BF16),
            pltpu.VMEM((128, 64), BF16),
            pltpu.VMEM((64, 256), BF16),
            pltpu.VMEM((128, 256), F32),
            pltpu.VMEM((64, 64), BF16),
            pltpu.VMEM((64, 64), BF16),
            pltpu.VMEM((64, 64), BF16),
            pltpu.VMEM((2, 256, LANES), F32),
            pltpu.VMEM((256, LANES), F32),
            pltpu.VMEM((LAYERS, 32, LANES), F32),
            pltpu.VMEM((256, LANES), F32),
            pltpu.VMEM((LAYERS, 32, LANES), F32),
            pltpu.VMEM((32, LANES), F32),
            pltpu.VMEM((32, LANES), F32),
            dma, dma((2,)), dma((SLOTS,)), dma((SLOTS,)),
            dma((SLOTS, 3)), dma((SLOTS, 3)), dma((SLOTS, 2)), dma((SLOTS, 2)), dma((SLOTS, 2)), dma((SLOTS, 2)),
            dma((SLOTS, 3)), dma((SLOTS, 3)), dma, dma, dma((LAYERS,)), dma((LAYERS,)), dma, dma,
        ],
        compiler_params=pltpu.CompilerParams(
            collective_id=0, has_side_effects=True, vmem_limit_bytes=62 * 2**20
        ),
        name="influence_scores",
    )(train_grads, query_pre, basis_in, basis_out)


def solution(mesh):
    placed = (
        P("query", "layer", None),
        P("query", "layer", None),
        P("layer", None, None),
        P("layer", None, None),
    )
    return jax.shard_map(
        shards, mesh=mesh, in_specs=placed, out_specs=P("layer", "query"), check_vma=False
    )
```

time: 809 us -> 197 us (0.24)
  waiting for transfers between devices: 535 us -> 0 us
  Pallas kernels: 0 us -> 176 us
  local copies, waits for them, and re-layouts: 123 us -> 20.2 us
  matrix products: 100 us -> 0 us
  starting transfers between devices: 33.2 us -> 0 us
  between operations: 13.4 us -> 0.01 us
    ppermute x15 -> x0, waiting for transfers between devices: 441 us -> none  [from_behind(): return lax.ppermute(value, axis, pairs)]
    pallas_call x0 -> x1, Pallas kernels: none -> 176 us  [shards(): pl.pallas_call(kernel, out_shape=jax.ShapeDtypeStruct((32, WIDTH), F32),...]
    reshape x5 -> x0, local copies, waits for them, and re-layouts: 100 us -> none  [the longest x2 57.5 us: shards(): query_pre.reshape(query_rows, modules, width, width)]
    dot_general x17 -> x0, matrix products: 100 us -> none  [the longest x16 90.3 us: score_block(): jnp.einsum('emk,qmk->eq', rotated, query_pre, preferred_element_type=jnp....]
    reduce_scatter x1 -> x0, waiting for transfers between devices: 94.2 us -> none  [shards(): return lax.psum_scatter(totals, 'layer', scatter_dimension=0, tiled=True)]
    ppermute x15 -> x0, starting transfers between devices: 33.2 us -> none  [from_behind(): return lax.ppermute(value, axis, pairs)]
    while x15 -> x0, local copies, waits for them, and re-layouts: 22.3 us -> none
    unnamed x10 -> x3, local copies, waits for them, and re-layouts: 0.67 us -> 20.2 us
  transfers between devices with their start and end apart: 16 -> 0, of which waited for: 16 -> 0; matrix products, arithmetic and copies ran while one was open for 0% -> 0% of each run, Pallas kernels for 0% -> 0%
where the time goes in v1:
time: 197 us
  Pallas kernels  176 us (89%)
  local copies, waits for them, and re-layouts  20.2 us (10%)
    pallas_call x1, Pallas kernels, shards(): pl.pallas_call(kernel, out_shape=jax.ShapeDtypeStruct((32, WIDTH), F32),...  176 us
    unnamed x3, local copies, waits for them, and re-layouts  20.2 us

profile of v1, /device:TPU:1, one launch (start us, length us, event | category | flops | bytes accessed | tf_op | source)
XLA Modules:
  0.0 196.5 jit_solution(588336728320607630)
XLA Ops:
  0.0 4.9 %copy.5.train_hbm = bf16[16,20,4096]{2,1,0:T(8,128)(2,1)} copy(bf16[16,20,4096]{2,0,1:T(8,128)(2,1)} %param.4) | data formatting | bytes 5242880 | tf_op args[0]
  4.9 13.9 %copy.6.query_hbm = bf16[64,20,4096]{2,1,0:T(8,128)(2,1)} copy(bf16[64,20,4096]{2,0,1:T(8,128)(2,1)} %param.5) | data formatting | bytes 20971520 | tf_op args[1]
  18.8 176.4 %influence_scores.1 = f32[32,64]{1,0:T(8,128)} custom-call(bf16[16,20,4096]{2,1,0:T(8,128)(2,1)} %copy.5.train_hbm, bf16[64,20,4096]{2,1,0:T(8,128)(2,1)} %copy.6.query_hbm, bf16[20,64,64]{2,1,0:T(8,128)(2,1)} %inner_ref.1, bf16[20,64,64]{2,1,0:T(8,128)(2,1)} %outer_ref.1), custom_call_target="tpu_custom_call" | custom-call | tf_op jit(solution)/shard_map/influence_scores/pallas_call | solution.py:402
  195.2 1.3 copy.8

commit v2 on v1

--- a/solution.py
+++ b/solution.py
@@ -13,14 +13,12 @@
 FLAT = WIDTH * WIDTH
 MODULES = 20
 OWN_TRAIN = 16
-OWN_QUERY = 64
 LAYERS = 8
 DEPTH = 4
 PAIR_SLOTS = 3
 COLUMN_SLOTS = 4
 SLOTS = PAIR_SLOTS + COLUMN_SLOTS
 LANES = 128
-CHUNKS = FLAT // LANES
 PARTNERS = ((0, 1), (1, 0), (1, 1))
 
 
@@ -42,10 +40,10 @@
 
 def kernel(
     train_hbm, query_hbm, inner_ref, outer_ref, out_ref,
-    train, query, padded, padded_query, swapped, rotated, queries, blocks, pair_queries, column_queries,
+    train, rotated, blocks, pair_queries, column_queries,
     swap, spread_rows, spread_lanes, keep, columns_of, rows_even, rows_odd,
     pair_scores, column_scores, mine, theirs, gathered, total, sib_total,
-    train_sem, query_sem, local_sem, local_query_sem,
+    train_sem, local_sem, local_query_sem,
     block_send, block_recv, ring_send, ring_recv, half_send, half_recv,
     query_send, query_recv, pair_send, pair_recv, layer_send, layer_recv, core_send, core_recv,
 ):
@@ -64,16 +62,17 @@
     def at_ring(step):
         return (layer, ((z + step + DEPTH) % DEPTH) * 4 + here)
 
-    load_train = pltpu.make_async_copy(train_hbm, train, train_sem)
-    load_train.start()
-
-    def load_query(part):
-        return pltpu.make_async_copy(
-            query_hbm.at[pl.ds(part * 16, 16)], query.at[part % 2], query_sem.at[part % 2]
-        )
-
-    load_query(0).start()
-    load_query(1).start()
+    def load_train(m):
+        return pltpu.make_async_copy(train_hbm.at[m], train.at[m], train_sem.at[m])
+
+    def each_module(first, last, step):
+        def body(m, carry):
+            step(m)
+            return carry
+
+        lax.fori_loop(first, last, body, 0)
+
+    each_module(0, MODULES, lambda m: load_train(m).start())
 
     barrier = pltpu.get_barrier_semaphore()
     for partner in PARTNERS:
@@ -98,90 +97,52 @@
     columns_of[...] = one_hot(col == 2 * (row % 32) + row // 32)
     rows_even[...] = one_hot(row == 2 * (col % 32) + col // 32)
     rows_odd[...] = one_hot(row == 2 * (col % 32) + 1 - col // 32)
-    padded[...] = jnp.zeros_like(padded)
-    padded_query[...] = jnp.zeros_like(padded_query)
 
     pl.semaphore_wait(barrier, len(PARTNERS) + 2 + LAYERS - 1)
 
-    def store_swapped(first, count, example, value):
-        pieces = jnp.concatenate(
-            [
-                jnp.concatenate(
-                    [value[:, (16 * half + c) * LANES:(16 * half + c + 1) * LANES] for c in range(16)], axis=0
-                )
-                for half in range(2)
-            ],
-            axis=1,
-        )
-        turned = dot(swap[0:16 * count, :], pieces).astype(BF16)
-        for m in range(count):
-            for half in range(2):
-                swapped[first + m, example, 16 * half:16 * half + 16, :] = turned[
-                    16 * m:16 * m + 16, half * LANES:(half + 1) * LANES
-                ]
-
-    def turn_train(example, carry):
-        store_swapped(0, 16, example, train[example, 0:16, :])
-        return carry
-
-    def turn_train_rest(example, carry):
-        padded[0:4, :] = train[example, 16:20, :]
-        store_swapped(16, 4, example, padded[...])
-        return carry
-
-    def rotate(m, carry):
+    def side_by_side(pieces):
+        return jnp.concatenate(pieces, axis=1)
+
+    def stack(pieces):
+        return jnp.concatenate(pieces, axis=0)
+
+    def swap_rows(tile):
+        pieces = side_by_side([stack([tile(16 * half + c) for c in range(16)]) for half in range(2)])
+        return dot(swap[...], pieces).astype(BF16)
+
+    def rotate(m):
         inner = dot(dot(spread_rows[...], inner_ref[m]).astype(BF16), spread_lanes[...])
         inner = (inner * keep[...]).astype(BF16)
         turned = dot_t(columns_of[...], outer_ref[m]).astype(BF16)
         outer = jnp.where(
             iota((64, 64), 0) < 32, dot(turned, rows_even[...]), dot(turned, rows_odd[...])
         ).astype(BF16)
-        half = dot(swapped[m].reshape(512, LANES), inner).astype(BF16)
-        stacked = jnp.concatenate(
+        load_train(m).wait()
+        grads = train[m]
+        rows = swap_rows(lambda c: grads[:, c * LANES:(c + 1) * LANES])
+        matrices = stack(
+            [rows[16 * e:16 * e + 16, h * LANES:(h + 1) * LANES] for e in range(OWN_TRAIN) for h in range(2)]
+        )
+        half = dot(matrices, inner).astype(BF16)
+        stacked = stack(
             [
-                jnp.concatenate(
-                    [half[32 * e:32 * e + 32, h * LANES:(h + 1) * LANES] for e in range(OWN_TRAIN)], axis=1
-                )
+                side_by_side([half[32 * e:32 * e + 32, h * LANES:(h + 1) * LANES] for e in range(OWN_TRAIN)])
                 for h in range(2)
-            ],
-            axis=0,
+            ]
         )
         both = dot(outer, stacked)
         first = iota((32, OWN_TRAIN * LANES), 1) % LANES < WIDTH
         result = jnp.where(first, both[:32], both[32:]).astype(BF16)
-        pieces = jnp.concatenate(
+        pieces = side_by_side(
             [
-                jnp.concatenate(
-                    [result[16 * h:16 * h + 16, e * LANES:(e + 1) * LANES] for e in range(OWN_TRAIN)], axis=0
-                )
+                stack([result[16 * h:16 * h + 16, e * LANES:(e + 1) * LANES] for e in range(OWN_TRAIN)])
                 for h in range(2)
-            ],
-            axis=1,
+            ]
         )
         final = dot(swap[...], pieces).astype(BF16)
-        rotated[m] = jnp.concatenate(
-            [final[16 * c:16 * c + 16, h * LANES:(h + 1) * LANES] for h in range(2) for c in range(16)], axis=1
-        )
-        return carry
-
-    def turn_query(part):
-        load_query(part).wait()
-        slot = part % 2
-        rows = pl.ds(pl.multiple_of(part * 16, 16), 16)
-
-        def lanes_step(step, carry):
-            lanes = pl.ds(pl.multiple_of(step * 256, 256), 256)
-            turned = dot(swap[...], query[slot, :, 0:16, lanes].reshape(256, 256)).astype(BF16)
-            for m in range(16):
-                queries[m, rows, lanes] = turned[16 * m:16 * m + 16]
-            for q in range(16):
-                padded_query[q, 0:4, :] = query[slot, q, 16:20, lanes]
-            turned = dot(swap[0:64, :], padded_query[...].reshape(256, 256)).astype(BF16)
-            for m in range(4):
-                queries[16 + m, rows, lanes] = turned[16 * m:16 * m + 16]
-            return carry
-
-        lax.fori_loop(0, FLAT // 256, lanes_step, 0)
+        rotated[m] = side_by_side(
+            [final[16 * c:16 * c + 16, h * LANES:(h + 1) * LANES] for h in range(2) for c in range(16)]
+        )
 
     def block_copy(slot, partner):
         x, c, device = at_plane(*PARTNERS[partner])
@@ -223,16 +184,15 @@
             device_id_type=MESH,
         )
 
-    def query_copy(slot, partner, part=None):
+    def query_copy(slot, partner):
         x, c, device = at_plane(*PARTNERS[partner])
-        rows = pl.ds(0, 64) if part is None else pl.ds(16 * part, 16)
-        to = pl.ds(pl.multiple_of(core * 64, 64) if part is None else pl.multiple_of(core * 64 + part * 16, 16), 64 if part is None else 16)
+        to = pl.ds(pl.multiple_of(core * 64, 64), 64)
         if slot < PAIR_SLOTS:
             m, target = 4 * slot + 2 * x + c, pair_queries.at[slot, PARTNERS[partner][0], to]
         else:
             m, target = 6 + 2 * slot + c, column_queries.at[slot - PAIR_SLOTS, to]
         return pltpu.make_async_remote_copy(
-            src_ref=queries.at[m, rows],
+            src_ref=query_hbm.at[m],
             dst_ref=target,
             send_sem=query_send.at[slot, partner],
             recv_sem=query_recv.at[slot, partner],
@@ -246,7 +206,7 @@
             m, target = 4 * slot + here, pair_queries.at[slot, 0, to]
         else:
             m, target = 6 + 2 * slot + core, column_queries.at[slot - PAIR_SLOTS, to]
-        return pltpu.make_async_copy(queries.at[m], target, local_query_sem.at[slot])
+        return pltpu.make_async_copy(query_hbm.at[m], target, local_query_sem.at[slot])
 
     def send_blocks(slot):
         for partner in (1, 2, 0):
@@ -268,47 +228,22 @@
     def query_partners(slot):
         return (1, 2, 0) if slot < PAIR_SLOTS else (0,)
 
-    def send_queries(part):
-        for slot in range(PAIR_SLOTS):
-            for partner in query_partners(slot):
-                query_copy(slot, partner, part).start()
-
-    load_train.wait()
-    lax.fori_loop(0, OWN_TRAIN, turn_train, 0)
-    lax.fori_loop(0, 4, rotate, 0)
-    send_blocks(0)
-    lax.fori_loop(4, 8, rotate, 0)
-    send_blocks(1)
-    send_ring(0)
-    turn_query(0)
-    load_query(2).start()
-    send_queries(0)
-    lax.fori_loop(8, 12, rotate, 0)
-    send_blocks(2)
-    send_ring(1)
-    turn_query(1)
-    load_query(3).start()
-    send_queries(1)
-    lax.fori_loop(0, OWN_TRAIN, turn_train_rest, 0)
-    lax.fori_loop(12, 16, rotate, 0)
-    send_blocks(3)
-    send_blocks(4)
-    send_ring(2)
-    turn_query(2)
-    send_queries(2)
-    send_ring(3)
-    lax.fori_loop(16, 20, rotate, 0)
-    send_blocks(5)
-    send_blocks(6)
-    send_ring(4)
-    turn_query(3)
-    send_queries(3)
-    for slot in range(PAIR_SLOTS, SLOTS):
-        query_copy(slot, 0).start()
+    def send_queries(slot):
+        for partner in query_partners(slot):
+            query_copy(slot, partner).start()
+        own_query_copy(slot).start()
+
     for slot in range(SLOTS):
-        own_query_copy(slot).start()
-    send_ring(5)
-    send_ring(6)
+        if slot < PAIR_SLOTS:
+            each_module(4 * slot, 4 * slot + 4, rotate)
+        else:
+            each_module(6 + 2 * slot, 8 + 2 * slot, rotate)
+        send_blocks(slot)
+        if slot > 0:
+            send_ring(slot - 1)
+    for slot in range(SLOTS):
+        send_queries(slot)
+    send_ring(SLOTS - 1)
     for slot in range(SLOTS):
         send_half(slot)
 
@@ -321,7 +256,8 @@
 
     pair_scores[...] = jnp.zeros_like(pair_scores)
     column_scores[...] = jnp.zeros_like(column_scores)
-    for slot in range(PAIR_SLOTS):
+
+    def score_pair(slot):
         wait_blocks(slot)
 
         def pair_step(step, carry):
@@ -333,6 +269,22 @@
 
         lax.fori_loop(0, FLAT // 512, pair_step, 0)
 
+    def score_column(slot):
+        wait_blocks(slot)
+
+        def column_step(step, carry):
+            lanes = pl.ds(pl.multiple_of(step * 512, 512), 512)
+            rows = blocks[slot, :, :, lanes].reshape(256, 512)
+            column_scores[...] += dot_t(rows, column_queries[slot - PAIR_SLOTS, :, lanes])
+            return carry
+
+        lax.fori_loop(0, FLAT // 512, column_step, 0)
+
+    score_pair(0)
+    score_pair(1)
+    score_column(3)
+    score_column(4)
+    score_pair(2)
     cross = pltpu.make_async_remote_copy(
         src_ref=pair_scores.at[1],
         dst_ref=theirs,
@@ -342,16 +294,8 @@
         device_id_type=MESH,
     )
     cross.start()
-    for slot in range(PAIR_SLOTS, SLOTS):
-        wait_blocks(slot)
-
-        def column_step(step, carry):
-            lanes = pl.ds(pl.multiple_of(step * 512, 512), 512)
-            rows = blocks[slot, :, :, lanes].reshape(256, 512)
-            column_scores[...] += dot_t(rows, column_queries[slot - PAIR_SLOTS, :, lanes])
-            return carry
-
-        lax.fori_loop(0, FLAT // 512, column_step, 0)
+    score_column(5)
+    score_column(6)
     cross.wait_recv()
     mine[...] = (pair_scores[0] + column_scores[...] + theirs[...]).reshape(LAYERS, 32, LANES)
 
@@ -410,13 +354,8 @@
         ],
         out_specs=pl.BlockSpec(memory_space=pltpu.VMEM),
         scratch_shapes=[
-            pltpu.VMEM((OWN_TRAIN, MODULES, FLAT), BF16),
-            pltpu.VMEM((2, 16, MODULES, FLAT), BF16),
-            pltpu.VMEM((16, FLAT), BF16),
-            pltpu.VMEM((16, 16, 256), BF16),
-            pltpu.VMEM((MODULES, OWN_TRAIN, CHUNKS, LANES), BF16),
             pltpu.VMEM((MODULES, OWN_TRAIN, FLAT), BF16),
-            pltpu.VMEM((MODULES, OWN_QUERY, FLAT), BF16),
+            pltpu.VMEM((MODULES, OWN_TRAIN, FLAT), BF16),
             pltpu.VMEM((SLOTS, DEPTH, 64, FLAT), BF16),
             pltpu.VMEM((PAIR_SLOTS, 2, 128, FLAT), BF16),
             pltpu.VMEM((COLUMN_SLOTS, 128, FLAT), BF16),
@@ -434,7 +373,7 @@
             pltpu.VMEM((LAYERS, 32, LANES), F32),
             pltpu.VMEM((32, LANES), F32),
             pltpu.VMEM((32, LANES), F32),
-            dma, dma((2,)), dma((SLOTS,)), dma((SLOTS,)),
+            dma((MODULES,)), dma((SLOTS,)), dma((SLOTS,)),
             dma((SLOTS, 3)), dma((SLOTS, 3)), dma((SLOTS, 2)), dma((SLOTS, 2)), dma((SLOTS, 2)), dma((SLOTS, 2)),
             dma((SLOTS, 3)), dma((SLOTS, 3)), dma, dma, dma((LAYERS,)), dma((LAYERS,)), dma, dma,
         ],
@@ -442,7 +381,7 @@
             collective_id=0, has_side_effects=True, vmem_limit_bytes=62 * 2**20
         ),
         name="influence_scores",
-    )(train_grads, query_pre, basis_in, basis_out)
+    )(jnp.transpose(train_grads, (1, 0, 2)), jnp.transpose(query_pre, (1, 0, 2)), basis_in, basis_out)
 
 
 def solution(mesh):

time: 197 us -> 151 us (0.77)
  Pallas kernels: 176 us -> 150 us
  local copies, waits for them, and re-layouts: 20.2 us -> 1.32 us
    pallas_call x1, Pallas kernels: 176 us -> 150 us  [shards(): pl.pallas_call(kernel, out_shape=jax.ShapeDtypeStruct((32, WIDTH), F32),...]
    unnamed x3 -> x1, local copies, waits for them, and re-layouts: 20.2 us -> 1.32 us
where the time goes in v2:
time: 151 us
  Pallas kernels  150 us (99%)
    pallas_call x1, Pallas kernels, shards(): pl.pallas_call(kernel, out_shape=jax.ShapeDtypeStruct((32, WIDTH), F32),...  150 us

profile of v2, /device:TPU:1, one launch (start us, length us, event | category | flops | bytes accessed | tf_op | source)
XLA Modules:
  0.0 150.9 jit_solution(12766693814090628965)
XLA Ops:
  0.0 149.5 %influence_scores.1 = f32[32,64]{1,0:T(8,128)} custom-call(bf16[20,16,4096]{2,1,0:T(8,128)(2,1)} %bitcast.3, bf16[20,64,4096]{2,1,0:T(8,128)(2,1)} %bitcast.2, bf16[20,64,64]{2,1,0:T(8,128)(2,1)} %inner_ref.1, bf16[20,64,64]{2,1,0:T(8,128)(2,1)} %outer_ref.1), custom_call_target="tpu_custom_call" | custom-call | tf_op jit(solution)/shard_map/influence_scores/pallas_call | solution.py:346
  149.5 1.3 copy.6

commit v3 on v2

--- a/solution.py
+++ b/solution.py
@@ -18,6 +18,8 @@
 PAIR_SLOTS = 3
 COLUMN_SLOTS = 4
 SLOTS = PAIR_SLOTS + COLUMN_SLOTS
+FIRST = PAIR_SLOTS
+LAST = SLOTS - 1
 LANES = 128
 PARTNERS = ((0, 1), (1, 0), (1, 1))
 
@@ -39,13 +41,14 @@
 
 
 def kernel(
-    train_hbm, query_hbm, inner_ref, outer_ref, out_ref,
+    train_hbm, query_hbm, inner_hbm, outer_hbm, out_ref,
+    inner_ref, outer_ref,
     train, rotated, blocks, pair_queries, column_queries,
     swap, spread_rows, spread_lanes, keep, columns_of, rows_even, rows_odd,
-    pair_scores, column_scores, mine, theirs, gathered, total, sib_total,
-    train_sem, local_sem, local_query_sem,
-    block_send, block_recv, ring_send, ring_recv, half_send, half_recv,
-    query_send, query_recv, pair_send, pair_recv, layer_send, layer_recv, core_send, core_recv,
+    pair_scores, column_scores, theirs, packed, gathered,
+    basis_sem, train_sem, local_sem, local_query_sem,
+    block_send, block_recv, piece_send, piece_recv, ring_send, ring_recv, half_send, half_recv,
+    query_send, query_recv, pair_send, pair_recv, layer_send, layer_recv,
 ):
     layer = lax.axis_index("layer")
     place = lax.axis_index("query")
@@ -62,17 +65,9 @@
     def at_ring(step):
         return (layer, ((z + step + DEPTH) % DEPTH) * 4 + here)
 
-    def load_train(m):
-        return pltpu.make_async_copy(train_hbm.at[m], train.at[m], train_sem.at[m])
-
-    def each_module(first, last, step):
-        def body(m, carry):
-            step(m)
-            return carry
-
-        lax.fori_loop(first, last, body, 0)
-
-    each_module(0, MODULES, lambda m: load_train(m).start())
+    def at_layer(step, other_core):
+        c = 1 - core if other_core else core
+        return ((layer + step) % LAYERS, z * 4 + column * 2 + c)
 
     barrier = pltpu.get_barrier_semaphore()
     for partner in PARTNERS:
@@ -80,9 +75,28 @@
     for step in (1, -1):
         pl.semaphore_signal(barrier, inc=1, device_id=at_ring(step), device_id_type=MESH)
     for step in range(1, LAYERS):
-        pl.semaphore_signal(
-            barrier, inc=1, device_id=((layer + step) % LAYERS, place), device_id_type=MESH
-        )
+        for other in range(2):
+            pl.semaphore_signal(barrier, inc=1, device_id=at_layer(step, other), device_id_type=MESH)
+
+    def load_train(m):
+        return pltpu.make_async_copy(train_hbm.at[m], train.at[m], train_sem.at[m])
+
+    def each_module(first, last, step):
+        def body(m, carry):
+            step(m)
+            return carry
+
+        lax.fori_loop(first, last, body, 0)
+
+    base = 6 + 2 * FIRST
+    load_inner = pltpu.make_async_copy(inner_hbm, inner_ref, basis_sem.at[0])
+    load_outer = pltpu.make_async_copy(outer_hbm, outer_ref, basis_sem.at[1])
+    load_train(base + core).start()
+    load_inner.start()
+    load_outer.start()
+    load_train(base + 1 - core).start()
+    each_module(0, base, lambda m: load_train(m).start())
+    each_module(base + 2, MODULES, lambda m: load_train(m).start())
 
     row, col = iota((256, 256), 0), iota((256, 256), 1)
     swap[...] = one_hot((row // 16 == col % 16) & (row % 16 == col // 16))
@@ -98,8 +112,6 @@
     rows_even[...] = one_hot(row == 2 * (col % 32) + col // 32)
     rows_odd[...] = one_hot(row == 2 * (col % 32) + 1 - col // 32)
 
-    pl.semaphore_wait(barrier, len(PARTNERS) + 2 + LAYERS - 1)
-
     def side_by_side(pieces):
         return jnp.concatenate(pieces, axis=1)
 
@@ -110,14 +122,20 @@
         pieces = side_by_side([stack([tile(16 * half + c) for c in range(16)]) for half in range(2)])
         return dot(swap[...], pieces).astype(BF16)
 
-    def rotate(m):
+    def rotate(*modules):
+        for m in modules:
+            load_train(m).wait()
+        values = [rotation(m) for m in modules]
+        for m, value in zip(modules, values):
+            rotated[m] = value
+
+    def rotation(m):
         inner = dot(dot(spread_rows[...], inner_ref[m]).astype(BF16), spread_lanes[...])
         inner = (inner * keep[...]).astype(BF16)
         turned = dot_t(columns_of[...], outer_ref[m]).astype(BF16)
         outer = jnp.where(
             iota((64, 64), 0) < 32, dot(turned, rows_even[...]), dot(turned, rows_odd[...])
         ).astype(BF16)
-        load_train(m).wait()
         grads = train[m]
         rows = swap_rows(lambda c: grads[:, c * LANES:(c + 1) * LANES])
         matrices = stack(
@@ -140,7 +158,7 @@
             ]
         )
         final = dot(swap[...], pieces).astype(BF16)
-        rotated[m] = side_by_side(
+        return side_by_side(
             [final[16 * c:16 * c + 16, h * LANES:(h + 1) * LANES] for h in range(2) for c in range(16)]
         )
 
@@ -186,9 +204,9 @@
 
     def query_copy(slot, partner):
         x, c, device = at_plane(*PARTNERS[partner])
-        to = pl.ds(pl.multiple_of(core * 64, 64), 64)
+        to = pl.ds(pl.multiple_of(PARTNERS[partner][0] * 128 + core * 64, 64), 64)
         if slot < PAIR_SLOTS:
-            m, target = 4 * slot + 2 * x + c, pair_queries.at[slot, PARTNERS[partner][0], to]
+            m, target = 4 * slot + 2 * x + c, pair_queries.at[slot, to]
         else:
             m, target = 6 + 2 * slot + c, column_queries.at[slot - PAIR_SLOTS, to]
         return pltpu.make_async_remote_copy(
@@ -203,7 +221,7 @@
     def own_query_copy(slot):
         to = pl.ds(pl.multiple_of(core * 64, 64), 64)
         if slot < PAIR_SLOTS:
-            m, target = 4 * slot + here, pair_queries.at[slot, 0, to]
+            m, target = 4 * slot + here, pair_queries.at[slot, to]
         else:
             m, target = 6 + 2 * slot + core, column_queries.at[slot - PAIR_SLOTS, to]
         return pltpu.make_async_copy(query_hbm.at[m], target, local_query_sem.at[slot])
@@ -233,19 +251,71 @@
             query_copy(slot, partner).start()
         own_query_copy(slot).start()
 
-    for slot in range(SLOTS):
+    def piece_copy(source, way, held=None):
+        target = blocks.at[FIRST, z, pl.ds(pl.multiple_of(source * 16, 16), 16)]
+        return pltpu.make_async_remote_copy(
+            src_ref=target if held is None else held,
+            dst_ref=target,
+            send_sem=piece_send.at[source, way],
+            recv_sem=piece_recv.at[source, way],
+            device_id=at_ring(1 - 2 * way),
+            device_id_type=MESH,
+        )
+
+    def send_own_piece():
+        for way in range(2):
+            piece_copy(here, way, rotated.at[base + core]).start()
+        own_copy(FIRST).start()
+
+    def send_piece(partner):
+        block_copy(FIRST, partner).wait_recv()
+        x, c, _ = at_plane(*PARTNERS[partner])
+        for way in range(2):
+            piece_copy(2 * x + c, way).start()
+
+    def send_first_half():
+        for way in range(2):
+            for source in range(4):
+                piece_copy(source, way).wait_recv()
+            half_copy(FIRST, way).start()
+
+    def rotate_slot(slot):
         if slot < PAIR_SLOTS:
             each_module(4 * slot, 4 * slot + 4, rotate)
         else:
             each_module(6 + 2 * slot, 8 + 2 * slot, rotate)
         send_blocks(slot)
-        if slot > 0:
-            send_ring(slot - 1)
-    for slot in range(SLOTS):
-        send_queries(slot)
-    send_ring(SLOTS - 1)
-    for slot in range(SLOTS):
-        send_half(slot)
+
+    load_inner.wait()
+    load_outer.wait()
+    rotate(base, base + 1)
+    rotate(0, 1)
+    rotate(2, 3)
+    pl.semaphore_wait(barrier, len(PARTNERS) + 2 + 2 * (LAYERS - 1))
+    for partner in (0, 1, 2):
+        block_copy(FIRST, partner).start()
+    send_own_piece()
+    send_blocks(0)
+    for slot in range(PAIR_SLOTS, SLOTS):
+        own_query_copy(slot).start()
+        query_copy(slot, 0).start()
+    send_piece(0)
+    rotate(4, 5)
+    send_piece(1)
+    send_piece(2)
+    rotate(6, 7)
+    send_blocks(1)
+    send_ring(0)
+    rotate(8, 9)
+    rotate(10, 11)
+    send_blocks(2)
+    send_first_half()
+    for slot in (4, 5, 6):
+        rotate(6 + 2 * slot, 7 + 2 * slot)
+        send_blocks(slot)
+    send_queries(0)
+    send_ring(1)
+    own_copy(FIRST).wait()
 
     def wait_blocks(slot):
         for way in range(2):
@@ -259,32 +329,37 @@
 
     def score_pair(slot):
         wait_blocks(slot)
-
-        def pair_step(step, carry):
-            lanes = pl.ds(pl.multiple_of(step * 512, 512), 512)
-            rows = blocks[slot, :, :, lanes].reshape(256, 512)
-            for side in range(2):
-                pair_scores[side] += dot_t(rows, pair_queries[slot, side, :, lanes])
-            return carry
-
-        lax.fori_loop(0, FLAT // 512, pair_step, 0)
+        scores = dot_t(blocks[slot].reshape(256, FLAT), pair_queries[slot])
+        for side in range(2):
+            pair_scores[side] += scores[:, side * LANES:(side + 1) * LANES]
 
     def score_column(slot):
         wait_blocks(slot)
-
-        def column_step(step, carry):
-            lanes = pl.ds(pl.multiple_of(step * 512, 512), 512)
-            rows = blocks[slot, :, :, lanes].reshape(256, 512)
-            column_scores[...] += dot_t(rows, column_queries[slot - PAIR_SLOTS, :, lanes])
-            return carry
-
-        lax.fori_loop(0, FLAT // 512, column_step, 0)
-
+        column_scores[...] += dot_t(blocks[slot].reshape(256, FLAT), column_queries[slot - PAIR_SLOTS])
+
+    def score_part(step):
+        source = (z + step) % DEPTH
+        rows = pl.ds(pl.multiple_of(source * 64, 64), 64)
+        column_scores[rows, :] += dot_t(blocks[LAST, source], column_queries[LAST - PAIR_SLOTS])
+
+    send_half(0)
+    send_ring(2)
+    score_column(3)
+    send_half(1)
+    send_ring(4)
+    send_queries(1)
+    send_half(2)
+    send_ring(5)
+    send_queries(2)
+    send_half(4)
+    send_ring(6)
     score_pair(0)
+    send_half(5)
     score_pair(1)
-    score_column(3)
     score_column(4)
+    send_half(6)
     score_pair(2)
+
     cross = pltpu.make_async_remote_copy(
         src_ref=pair_scores.at[1],
         dst_ref=theirs,
@@ -295,41 +370,44 @@
     )
     cross.start()
     score_column(5)
-    score_column(6)
+    query_copy(LAST, 0).wait_recv()
+    own_query_copy(LAST).wait()
+    for step in (0, 1, 3):
+        score_part(step)
+    for way in range(2):
+        half_copy(LAST, way).wait_recv()
+    score_part(2)
     cross.wait_recv()
-    mine[...] = (pair_scores[0] + column_scores[...] + theirs[...]).reshape(LAYERS, 32, LANES)
-
-    def layer_copy(step):
-        return pltpu.make_async_remote_copy(
-            src_ref=mine.at[(layer + step) % LAYERS],
-            dst_ref=gathered.at[step],
-            send_sem=layer_send.at[step],
-            recv_sem=layer_recv.at[step],
-            device_id=((layer + step) % LAYERS, place),
-            device_id_type=MESH,
-        )
-
-    for step in range(1, LAYERS):
-        layer_copy(step).start()
-    total[...] = mine[layer]
-    for step in range(1, LAYERS):
-        layer_copy(step).wait_recv()
-        total[...] += gathered[step]
-    between = pltpu.make_async_remote_copy(
-        src_ref=total,
-        dst_ref=sib_total,
-        send_sem=core_send,
-        recv_sem=core_recv,
-        device_id=at_plane(0, 1)[2],
-        device_id_type=MESH,
-    )
-    between.start()
-    between.wait()
-    both = total[...] + sib_total[...]
-    out_ref[...] = jnp.where(core == 0, both[:, :WIDTH], both[:, WIDTH:])
-
-    for step in range(1, LAYERS):
-        layer_copy(step).wait_send()
+    own = pair_scores[0] + column_scores[...] + theirs[...]
+    moved = pltpu.roll(own, WIDTH, 1)
+    left = iota((LAYERS, 16, LANES), 2) < WIDTH
+    own = own.reshape(LAYERS, 2, 16, LANES)
+    moved = moved.reshape(LAYERS, 2, 16, LANES)
+    packed[:, 0] = jnp.where(left, own[:, 0], moved[:, 1])
+    packed[:, 1] = jnp.where(left, moved[:, 0], own[:, 1])
+
+    def layer_copy(step, other):
+        return pltpu.make_async_remote_copy(
+            src_ref=packed.at[(layer + step) % LAYERS, 1 - core if other else core],
+            dst_ref=gathered.at[step, other],
+            send_sem=layer_send.at[step, other],
+            recv_sem=layer_recv.at[step, other],
+            device_id=at_layer(step, other),
+            device_id_type=MESH,
+        )
+
+    others = [(step, other) for step in range(LAYERS) for other in range(2) if step or other]
+    for step, other in others:
+        layer_copy(step, other).start()
+    total = packed[layer, core]
+    for step, other in others:
+        layer_copy(step, other).wait_recv()
+        total += gathered[step, other]
+    out_ref[0:16, :] = total[:, :WIDTH]
+    out_ref[16:32, :] = total[:, WIDTH:]
+
+    for step, other in others:
+        layer_copy(step, other).wait_send()
     cross.wait_send()
     for slot in range(SLOTS):
         for partner in range(3):
@@ -337,7 +415,11 @@
         for partner in query_partners(slot):
             query_copy(slot, partner).wait_send()
         for way in range(2):
-            ring_copy(slot, way).wait_send()
+            if slot == FIRST:
+                for source in range(4):
+                    piece_copy(source, way).wait_send()
+            else:
+                ring_copy(slot, way).wait_send()
             half_copy(slot, way).wait_send()
 
 
@@ -349,15 +431,17 @@
         in_specs=[
             pl.BlockSpec(memory_space=pl.ANY),
             pl.BlockSpec(memory_space=pl.ANY),
-            pl.BlockSpec(memory_space=pltpu.VMEM),
-            pl.BlockSpec(memory_space=pltpu.VMEM),
+            pl.BlockSpec(memory_space=pl.ANY),
+            pl.BlockSpec(memory_space=pl.ANY),
         ],
         out_specs=pl.BlockSpec(memory_space=pltpu.VMEM),
         scratch_shapes=[
+            pltpu.VMEM((MODULES, WIDTH, WIDTH), BF16),
+            pltpu.VMEM((MODULES, WIDTH, WIDTH), BF16),
             pltpu.VMEM((MODULES, OWN_TRAIN, FLAT), BF16),
             pltpu.VMEM((MODULES, OWN_TRAIN, FLAT), BF16),
             pltpu.VMEM((SLOTS, DEPTH, 64, FLAT), BF16),
-            pltpu.VMEM((PAIR_SLOTS, 2, 128, FLAT), BF16),
+            pltpu.VMEM((PAIR_SLOTS, 256, FLAT), BF16),
             pltpu.VMEM((COLUMN_SLOTS, 128, FLAT), BF16),
             pltpu.VMEM((256, 256), BF16),
             pltpu.VMEM((128, 64), BF16),
@@ -368,14 +452,12 @@
             pltpu.VMEM((64, 64), BF16),
             pltpu.VMEM((2, 256, LANES), F32),
             pltpu.VMEM((256, LANES), F32),
-            pltpu.VMEM((LAYERS, 32, LANES), F32),
             pltpu.VMEM((256, LANES), F32),
-            pltpu.VMEM((LAYERS, 32, LANES), F32),
-            pltpu.VMEM((32, LANES), F32),
-            pltpu.VMEM((32, LANES), F32),
-            dma((MODULES,)), dma((SLOTS,)), dma((SLOTS,)),
-            dma((SLOTS, 3)), dma((SLOTS, 3)), dma((SLOTS, 2)), dma((SLOTS, 2)), dma((SLOTS, 2)), dma((SLOTS, 2)),
-            dma((SLOTS, 3)), dma((SLOTS, 3)), dma, dma, dma((LAYERS,)), dma((LAYERS,)), dma, dma,
+            pltpu.VMEM((LAYERS, 2, 16, LANES), F32),
+            pltpu.VMEM((LAYERS, 2, 16, LANES), F32),
+            dma((2,)), dma((MODULES,)), dma((SLOTS,)), dma((SLOTS,)),
+            dma((SLOTS, 3)), dma((SLOTS, 3)), dma((4, 2)), dma((4, 2)), dma((SLOTS, 2)), dma((SLOTS, 2)), dma((SLOTS, 2)), dma((SLOTS, 2)),
+            dma((SLOTS, 3)), dma((SLOTS, 3)), dma, dma, dma((LAYERS, 2)), dma((LAYERS, 2)),
         ],
         compiler_params=pltpu.CompilerParams(
             collective_id=0, has_side_effects=True, vmem_limit_bytes=62 * 2**20

time: 151 us -> 143 us (0.947)
  Pallas kernels: 150 us -> 141 us
    pallas_call x1, Pallas kernels: 150 us -> 141 us  [shards(): pl.pallas_call(kernel, out_shape=jax.ShapeDtypeStruct((32, WIDTH), F32),...]
where the time goes in v3:
time: 143 us; the launch traced here: 142 us
  Pallas kernels  141 us (99%)
    pallas_call x1, Pallas kernels, shards(): pl.pallas_call(kernel, out_shape=jax.ShapeDtypeStruct((32, WIDTH), F32),...  141 us

profile of v3, /device:TPU:1, one launch (start us, length us, event | category | flops | bytes accessed | tf_op | source)
XLA Modules:
  0.0 142.5 jit_solution(3636971560883767887)
XLA Ops:
  0.0 141.1 %influence_scores.1 = f32[32,64]{1,0:T(8,128)} custom-call(bf16[20,16,4096]{2,1,0:T(8,128)(2,1)} %bitcast.3, bf16[20,64,4096]{2,1,0:T(8,128)(2,1)} %bitcast.2, bf16[20,64,64]{2,1,0:T(8,128)(2,1)} %inner_hbm.1, bf16[20,64,64]{2,1,0:T(8,128)(2,1)} %outer_hbm.1), custom_call_target="tpu_custom_call" | custom-call | tf_op jit(solution)/shard_map/influence_scores/pallas_call | solution.py:428
  141.1 1.3 copy.6

commit v4 on v3

--- a/solution.py
+++ b/solution.py
@@ -15,11 +15,13 @@
 OWN_TRAIN = 16
 LAYERS = 8
 DEPTH = 4
-PAIR_SLOTS = 3
-COLUMN_SLOTS = 4
-SLOTS = PAIR_SLOTS + COLUMN_SLOTS
-FIRST = PAIR_SLOTS
-LAST = SLOTS - 1
+SLOTS = 8
+FIRST = 3
+LAST = 6
+EXTRA = 7
+SHARED = 1024
+REST = FLAT - SHARED
+IN_PIECES = (FIRST, 0)
 LANES = 128
 PARTNERS = ((0, 1), (1, 0), (1, 1))
 
@@ -43,7 +45,7 @@
 def kernel(
     train_hbm, query_hbm, inner_hbm, outer_hbm, out_ref,
     inner_ref, outer_ref,
-    train, rotated, blocks, pair_queries, column_queries,
+    train, rotated, full_blocks, rest_blocks, extra_blocks, pair_queries, extra_queries, column_queries, rest_queries,
     swap, spread_rows, spread_lanes, keep, columns_of, rows_even, rows_odd,
     pair_scores, column_scores, theirs, packed, gathered,
     basis_sem, train_sem, local_sem, local_query_sem,
@@ -162,12 +164,37 @@
             [final[16 * c:16 * c + 16, h * LANES:(h + 1) * LANES] for h in range(2) for c in range(16)]
         )
 
+    def is_pair(slot):
+        return slot < 3 or slot == EXTRA
+
+    def module_of(slot, x, c):
+        if slot == EXTRA:
+            return 16 + 2 * x + c
+        return 4 * slot + 2 * x + c if is_pair(slot) else 6 + 2 * slot + c
+
+    def entries(slot):
+        if slot == EXTRA:
+            return pl.ds(0, SHARED)
+        return pl.ds(SHARED, REST) if slot >= 5 else pl.ds(0, FLAT)
+
+    def blocks(slot):
+        if slot == EXTRA:
+            return extra_blocks
+        return rest_blocks.at[slot - 5] if slot >= 5 else full_blocks.at[slot]
+
+    def queries(slot):
+        if is_pair(slot):
+            return extra_queries if slot == EXTRA else pair_queries.at[slot]
+        return rest_queries.at[slot - 5] if slot >= 5 else column_queries.at[slot - 3]
+
+    def own_rows(count, first):
+        return pl.ds(pl.multiple_of(first * count, count), count)
+
     def block_copy(slot, partner):
         x, c, device = at_plane(*PARTNERS[partner])
-        m = 4 * slot + 2 * x + c if slot < PAIR_SLOTS else 6 + 2 * slot + c
         return pltpu.make_async_remote_copy(
-            src_ref=rotated.at[m],
-            dst_ref=blocks.at[slot, z, pl.ds(pl.multiple_of(here * 16, 16), 16)],
+            src_ref=rotated.at[module_of(slot, x, c), :, entries(slot)],
+            dst_ref=blocks(slot).at[z, own_rows(16, here)],
             send_sem=block_send.at[slot, partner],
             recv_sem=block_recv.at[slot, partner],
             device_id=device,
@@ -175,15 +202,16 @@
         )
 
     def own_copy(slot):
-        m = 4 * slot + here if slot < PAIR_SLOTS else 6 + 2 * slot + core
         return pltpu.make_async_copy(
-            rotated.at[m], blocks.at[slot, z, pl.ds(pl.multiple_of(here * 16, 16), 16)], local_sem.at[slot]
+            rotated.at[module_of(slot, column, core), :, entries(slot)],
+            blocks(slot).at[z, own_rows(16, here)],
+            local_sem.at[slot],
         )
 
     def ring_copy(slot, way):
         return pltpu.make_async_remote_copy(
-            src_ref=blocks.at[slot, z],
-            dst_ref=blocks.at[slot, z],
+            src_ref=blocks(slot).at[z],
+            dst_ref=blocks(slot).at[z],
             send_sem=ring_send.at[slot, way],
             recv_sem=ring_recv.at[slot, way],
             device_id=at_ring(1 - 2 * way),
@@ -192,7 +220,7 @@
 
     def half_copy(slot, way):
         source = (z + DEPTH - 1 + 2 * way) % DEPTH
-        half = blocks.at[slot, source, pl.ds(32 * way, 32)]
+        half = blocks(slot).at[source, pl.ds(32 * way, 32)]
         return pltpu.make_async_remote_copy(
             src_ref=half,
             dst_ref=half,
@@ -204,14 +232,9 @@
 
     def query_copy(slot, partner):
         x, c, device = at_plane(*PARTNERS[partner])
-        to = pl.ds(pl.multiple_of(PARTNERS[partner][0] * 128 + core * 64, 64), 64)
-        if slot < PAIR_SLOTS:
-            m, target = 4 * slot + 2 * x + c, pair_queries.at[slot, to]
-        else:
-            m, target = 6 + 2 * slot + c, column_queries.at[slot - PAIR_SLOTS, to]
         return pltpu.make_async_remote_copy(
-            src_ref=query_hbm.at[m],
-            dst_ref=target,
+            src_ref=query_hbm.at[module_of(slot, x, c), :, entries(slot)],
+            dst_ref=queries(slot).at[own_rows(64, PARTNERS[partner][0] * 2 + core)],
             send_sem=query_send.at[slot, partner],
             recv_sem=query_recv.at[slot, partner],
             device_id=device,
@@ -219,17 +242,44 @@
         )
 
     def own_query_copy(slot):
-        to = pl.ds(pl.multiple_of(core * 64, 64), 64)
-        if slot < PAIR_SLOTS:
-            m, target = 4 * slot + here, pair_queries.at[slot, to]
-        else:
-            m, target = 6 + 2 * slot + core, column_queries.at[slot - PAIR_SLOTS, to]
-        return pltpu.make_async_copy(query_hbm.at[m], target, local_query_sem.at[slot])
+        return pltpu.make_async_copy(
+            query_hbm.at[module_of(slot, column, core), :, entries(slot)],
+            queries(slot).at[own_rows(64, core)],
+            local_query_sem.at[slot],
+        )
+
+    def piece_copy(slot, source, way, held=None):
+        target = blocks(slot).at[z, own_rows(16, source)]
+        return pltpu.make_async_remote_copy(
+            src_ref=target if held is None else held,
+            dst_ref=target,
+            send_sem=piece_send.at[IN_PIECES.index(slot), source, way],
+            recv_sem=piece_recv.at[IN_PIECES.index(slot), source, way],
+            device_id=at_ring(1 - 2 * way),
+            device_id_type=MESH,
+        )
+
+    def query_partners(slot):
+        return (1, 2, 0) if is_pair(slot) else (0,)
+
+    def send_queries(slot):
+        for partner in query_partners(slot):
+            query_copy(slot, partner).start()
+        own_query_copy(slot).start()
 
     def send_blocks(slot):
         for partner in (1, 2, 0):
             block_copy(slot, partner).start()
+        if slot in IN_PIECES:
+            for way in range(2):
+                piece_copy(slot, here, way, rotated.at[module_of(slot, column, core)]).start()
         own_copy(slot).start()
+
+    def send_piece(slot, partner):
+        block_copy(slot, partner).wait_recv()
+        x, c, _ = at_plane(*PARTNERS[partner])
+        for way in range(2):
+            piece_copy(slot, 2 * x + c, way).start()
 
     def send_ring(slot):
         for partner in range(3):
@@ -240,86 +290,54 @@
 
     def send_half(slot):
         for way in range(2):
-            ring_copy(slot, way).wait_recv()
+            if slot in IN_PIECES:
+                for source in range(4):
+                    piece_copy(slot, source, way).wait_recv()
+            else:
+                ring_copy(slot, way).wait_recv()
             half_copy(slot, way).start()
-
-    def query_partners(slot):
-        return (1, 2, 0) if slot < PAIR_SLOTS else (0,)
-
-    def send_queries(slot):
-        for partner in query_partners(slot):
-            query_copy(slot, partner).start()
-        own_query_copy(slot).start()
-
-    def piece_copy(source, way, held=None):
-        target = blocks.at[FIRST, z, pl.ds(pl.multiple_of(source * 16, 16), 16)]
-        return pltpu.make_async_remote_copy(
-            src_ref=target if held is None else held,
-            dst_ref=target,
-            send_sem=piece_send.at[source, way],
-            recv_sem=piece_recv.at[source, way],
-            device_id=at_ring(1 - 2 * way),
-            device_id_type=MESH,
-        )
-
-    def send_own_piece():
-        for way in range(2):
-            piece_copy(here, way, rotated.at[base + core]).start()
-        own_copy(FIRST).start()
-
-    def send_piece(partner):
-        block_copy(FIRST, partner).wait_recv()
-        x, c, _ = at_plane(*PARTNERS[partner])
-        for way in range(2):
-            piece_copy(2 * x + c, way).start()
-
-    def send_first_half():
-        for way in range(2):
-            for source in range(4):
-                piece_copy(source, way).wait_recv()
-            half_copy(FIRST, way).start()
-
-    def rotate_slot(slot):
-        if slot < PAIR_SLOTS:
-            each_module(4 * slot, 4 * slot + 4, rotate)
-        else:
-            each_module(6 + 2 * slot, 8 + 2 * slot, rotate)
-        send_blocks(slot)
 
     load_inner.wait()
     load_outer.wait()
     rotate(base, base + 1)
+    pl.semaphore_wait(barrier, len(PARTNERS) + 2 + 2 * (LAYERS - 1))
+    send_blocks(3)
     rotate(0, 1)
+    send_piece(3, 0)
     rotate(2, 3)
-    pl.semaphore_wait(barrier, len(PARTNERS) + 2 + 2 * (LAYERS - 1))
-    for partner in (0, 1, 2):
-        block_copy(FIRST, partner).start()
-    send_own_piece()
     send_blocks(0)
-    for slot in range(PAIR_SLOTS, SLOTS):
-        own_query_copy(slot).start()
-        query_copy(slot, 0).start()
-    send_piece(0)
+    send_piece(3, 1)
     rotate(4, 5)
-    send_piece(1)
-    send_piece(2)
+    send_piece(3, 2)
+    send_piece(0, 0)
     rotate(6, 7)
     send_blocks(1)
-    send_ring(0)
+    send_piece(0, 1)
     rotate(8, 9)
+    send_piece(0, 2)
     rotate(10, 11)
     send_blocks(2)
-    send_first_half()
-    for slot in (4, 5, 6):
-        rotate(6 + 2 * slot, 7 + 2 * slot)
-        send_blocks(slot)
+    for slot in (3, 4, 5, 6):
+        send_queries(slot)
+    send_half(3)
+    rotate(16, 17)
+    rotate(18, 19)
+    send_blocks(7)
+    rotate(14, 15)
+    send_blocks(4)
+    send_blocks(5)
+    send_blocks(6)
     send_queries(0)
     send_ring(1)
-    own_copy(FIRST).wait()
 
     def wait_blocks(slot):
         for way in range(2):
             half_copy(slot, way).wait_recv()
+        if slot in IN_PIECES:
+            own_copy(slot).wait()
+        wait_queries(slot)
+
+    def wait_queries(slot):
         for partner in query_partners(slot):
             query_copy(slot, partner).wait_recv()
         own_query_copy(slot).wait()
@@ -327,38 +345,42 @@
     pair_scores[...] = jnp.zeros_like(pair_scores)
     column_scores[...] = jnp.zeros_like(column_scores)
 
-    def score_pair(slot):
+    def score(slot):
         wait_blocks(slot)
-        scores = dot_t(blocks[slot].reshape(256, FLAT), pair_queries[slot])
-        for side in range(2):
-            pair_scores[side] += scores[:, side * LANES:(side + 1) * LANES]
-
-    def score_column(slot):
-        wait_blocks(slot)
-        column_scores[...] += dot_t(blocks[slot].reshape(256, FLAT), column_queries[slot - PAIR_SLOTS])
+        rows = blocks(slot)[...]
+        scores = dot_t(rows.reshape(256, rows.shape[2]), queries(slot)[...])
+        if is_pair(slot):
+            for side in range(2):
+                pair_scores[side] += scores[:, side * LANES:(side + 1) * LANES]
+        else:
+            column_scores[...] += scores
 
     def score_part(step):
         source = (z + step) % DEPTH
         rows = pl.ds(pl.multiple_of(source * 64, 64), 64)
-        column_scores[rows, :] += dot_t(blocks[LAST, source], column_queries[LAST - PAIR_SLOTS])
+        column_scores[rows, :] += dot_t(blocks(LAST)[source], queries(LAST)[...])
 
     send_half(0)
     send_ring(2)
-    score_column(3)
+    score(3)
     send_half(1)
+    send_ring(7)
+    send_queries(1)
+    send_queries(7)
+    send_half(2)
     send_ring(4)
-    send_queries(1)
-    send_half(2)
+    send_queries(2)
+    send_half(7)
     send_ring(5)
-    send_queries(2)
+    score(0)
     send_half(4)
     send_ring(6)
-    score_pair(0)
+    score(1)
     send_half(5)
-    score_pair(1)
-    score_column(4)
+    score(4)
+    score(7)
     send_half(6)
-    score_pair(2)
+    score(2)
 
     cross = pltpu.make_async_remote_copy(
         src_ref=pair_scores.at[1],
@@ -369,9 +391,8 @@
         device_id_type=MESH,
     )
     cross.start()
-    score_column(5)
-    query_copy(LAST, 0).wait_recv()
-    own_query_copy(LAST).wait()
+    score(5)
+    wait_queries(LAST)
     for step in (0, 1, 3):
         score_part(step)
     for way in range(2):
@@ -415,9 +436,9 @@
         for partner in query_partners(slot):
             query_copy(slot, partner).wait_send()
         for way in range(2):
-            if slot == FIRST:
+            if slot in IN_PIECES:
                 for source in range(4):
-                    piece_copy(source, way).wait_send()
+                    piece_copy(slot, source, way).wait_send()
             else:
                 ring_copy(slot, way).wait_send()
             half_copy(slot, way).wait_send()
@@ -440,9 +461,13 @@
             pltpu.VMEM((MODULES, WIDTH, WIDTH), BF16),
             pltpu.VMEM((MODULES, OWN_TRAIN, FLAT), BF16),
             pltpu.VMEM((MODULES, OWN_TRAIN, FLAT), BF16),
-            pltpu.VMEM((SLOTS, DEPTH, 64, FLAT), BF16),
-            pltpu.VMEM((PAIR_SLOTS, 256, FLAT), BF16),
-            pltpu.VMEM((COLUMN_SLOTS, 128, FLAT), BF16),
+            pltpu.VMEM((5, DEPTH, 64, FLAT), BF16),
+            pltpu.VMEM((2, DEPTH, 64, REST), BF16),
+            pltpu.VMEM((DEPTH, 64, SHARED), BF16),
+            pltpu.VMEM((3, 256, FLAT), BF16),
+            pltpu.VMEM((256, SHARED), BF16),
+            pltpu.VMEM((2, 128, FLAT), BF16),
+            pltpu.VMEM((2, 128, REST), BF16),
             pltpu.VMEM((256, 256), BF16),
             pltpu.VMEM((128, 64), BF16),
             pltpu.VMEM((64, 256), BF16),
@@ -456,7 +481,7 @@
             pltpu.VMEM((LAYERS, 2, 16, LANES), F32),
             pltpu.VMEM((LAYERS, 2, 16, LANES), F32),
             dma((2,)), dma((MODULES,)), dma((SLOTS,)), dma((SLOTS,)),
-            dma((SLOTS, 3)), dma((SLOTS, 3)), dma((4, 2)), dma((4, 2)), dma((SLOTS, 2)), dma((SLOTS, 2)), dma((SLOTS, 2)), dma((SLOTS, 2)),
+            dma((SLOTS, 3)), dma((SLOTS, 3)), dma((2, 4, 2)), dma((2, 4, 2)), dma((SLOTS, 2)), dma((SLOTS, 2)), dma((SLOTS, 2)), dma((SLOTS, 2)),
             dma((SLOTS, 3)), dma((SLOTS, 3)), dma, dma, dma((LAYERS, 2)), dma((LAYERS, 2)),
         ],
         compiler_params=pltpu.CompilerParams(

time: 143 us -> 135 us (0.944)
  Pallas kernels: 141 us -> 134 us
    pallas_call x1, Pallas kernels: 141 us -> 134 us  [shards(): pl.pallas_call(kernel, out_shape=jax.ShapeDtypeStruct((32, WIDTH), F32),...]
where the time goes in v4:
time: 135 us
  Pallas kernels  134 us (99%)
    pallas_call x1, Pallas kernels, shards(): pl.pallas_call(kernel, out_shape=jax.ShapeDtypeStruct((32, WIDTH), F32),...  134 us

profile of v4, /device:TPU:1, one launch (start us, length us, event | category | flops | bytes accessed | tf_op | source)
XLA Modules:
  0.0 135.1 jit_solution(11672745067593813941)
XLA Ops:
  0.0 133.8 %influence_scores.1 = f32[32,64]{1,0:T(8,128)} custom-call(bf16[20,16,4096]{2,1,0:T(8,128)(2,1)} %bitcast.3, bf16[20,64,4096]{2,1,0:T(8,128)(2,1)} %bitcast.2, bf16[20,64,64]{2,1,0:T(8,128)(2,1)} %inner_hbm.1, bf16[20,64,64]{2,1,0:T(8,128)(2,1)} %outer_hbm.1), custom_call_target="tpu_custom_call" | custom-call | tf_op jit(solution)/shard_map/influence_scores/pallas_call | solution.py:449
  133.8 1.3 copy.6

commit v5 on v4

--- a/solution.py
+++ b/solution.py
@@ -22,6 +22,7 @@
 SHARED = 1024
 REST = FLAT - SHARED
 IN_PIECES = (FIRST, 0)
+FAR_FIRST = ((1, 2), (1, 1), (1, 3), (0, 2), (1, 0), (0, 1), (0, 3), (0, 0))
 LANES = 128
 PARTNERS = ((0, 1), (1, 0), (1, 1))
 
@@ -50,7 +51,7 @@
     pair_scores, column_scores, theirs, packed, gathered,
     basis_sem, train_sem, local_sem, local_query_sem,
     block_send, block_recv, piece_send, piece_recv, ring_send, ring_recv, half_send, half_recv,
-    query_send, query_recv, pair_send, pair_recv, layer_send, layer_recv,
+    query_send, query_recv, pair_send, pair_recv, layer_send, layer_recv, told,
 ):
     layer = lax.axis_index("layer")
     place = lax.axis_index("query")
@@ -67,18 +68,29 @@
     def at_ring(step):
         return (layer, ((z + step + DEPTH) % DEPTH) * 4 + here)
 
-    def at_layer(step, other_core):
+    def layer_at(over, step):
+        return (layer // 4 + over) % 2 * 4 + (layer + step) % 4
+
+    def at_layer(over, step, other_core):
         c = 1 - core if other_core else core
-        return ((layer + step) % LAYERS, z * 4 + column * 2 + c)
+        return (layer_at(over, step), z * 4 + column * 2 + c)
+
+    near = (at_layer(0, 1, 0), at_layer(0, 3, 0), at_layer(1, 0, 0), at_layer(0, 0, 1))
+
+    def tell(turn):
+        for device in near:
+            pl.semaphore_signal(told.at[turn], inc=1, device_id=device, device_id_type=MESH)
+
+    def hear(turn):
+        pl.semaphore_wait(told.at[turn], len(near))
 
     barrier = pltpu.get_barrier_semaphore()
     for partner in PARTNERS:
         pl.semaphore_signal(barrier, inc=1, device_id=at_plane(*partner)[2], device_id_type=MESH)
     for step in (1, -1):
         pl.semaphore_signal(barrier, inc=1, device_id=at_ring(step), device_id_type=MESH)
-    for step in range(1, LAYERS):
-        for other in range(2):
-            pl.semaphore_signal(barrier, inc=1, device_id=at_layer(step, other), device_id_type=MESH)
+    for device in near[:3]:
+        pl.semaphore_signal(barrier, inc=1, device_id=device, device_id_type=MESH)
 
     def load_train(m):
         return pltpu.make_async_copy(train_hbm.at[m], train.at[m], train_sem.at[m])
@@ -300,8 +312,9 @@
     load_inner.wait()
     load_outer.wait()
     rotate(base, base + 1)
-    pl.semaphore_wait(barrier, len(PARTNERS) + 2 + 2 * (LAYERS - 1))
+    pl.semaphore_wait(barrier, len(PARTNERS) + 2 + 3)
     send_blocks(3)
+    tell(0)
     rotate(0, 1)
     send_piece(3, 0)
     rotate(2, 3)
@@ -317,6 +330,8 @@
     send_piece(0, 2)
     rotate(10, 11)
     send_blocks(2)
+    hear(0)
+    tell(1)
     for slot in (3, 4, 5, 6):
         send_queries(slot)
     send_half(3)
@@ -329,6 +344,8 @@
     send_blocks(6)
     send_queries(0)
     send_ring(1)
+    hear(1)
+    tell(2)
 
     def wait_blocks(slot):
         for way in range(2):
@@ -360,21 +377,22 @@
         rows = pl.ds(pl.multiple_of(source * 64, 64), 64)
         column_scores[rows, :] += dot_t(blocks(LAST)[source], queries(LAST)[...])
 
+    send_ring(2)
     send_half(0)
-    send_ring(2)
-    score(3)
+    send_ring(7)
     send_half(1)
-    send_ring(7)
+    send_ring(4)
     send_queries(1)
     send_queries(7)
+    score(3)
+    hear(2)
     send_half(2)
-    send_ring(4)
+    send_ring(5)
     send_queries(2)
     send_half(7)
-    send_ring(5)
+    send_ring(6)
+    send_half(4)
     score(0)
-    send_half(4)
-    send_ring(6)
     score(1)
     send_half(5)
     score(4)
@@ -407,28 +425,21 @@
     packed[:, 0] = jnp.where(left, own[:, 0], moved[:, 1])
     packed[:, 1] = jnp.where(left, moved[:, 0], own[:, 1])
 
-    def layer_copy(step, other):
+    def layer_copy(over, step, other):
         return pltpu.make_async_remote_copy(
-            src_ref=packed.at[(layer + step) % LAYERS, 1 - core if other else core],
-            dst_ref=gathered.at[step, other],
-            send_sem=layer_send.at[step, other],
-            recv_sem=layer_recv.at[step, other],
-            device_id=at_layer(step, other),
+            src_ref=packed.at[layer_at(over, step), 1 - core if other else core],
+            dst_ref=gathered.at[over * 4 + step, other],
+            send_sem=layer_send.at[over * 4 + step, other],
+            recv_sem=layer_recv.at[over * 4 + step, other],
+            device_id=at_layer(over, step, other),
             device_id_type=MESH,
         )
 
-    others = [(step, other) for step in range(LAYERS) for other in range(2) if step or other]
-    for step, other in others:
-        layer_copy(step, other).start()
-    total = packed[layer, core]
-    for step, other in others:
-        layer_copy(step, other).wait_recv()
-        total += gathered[step, other]
-    out_ref[0:16, :] = total[:, :WIDTH]
-    out_ref[16:32, :] = total[:, WIDTH:]
-
-    for step, other in others:
-        layer_copy(step, other).wait_send()
+    others = [(over, step, other) for over, step in FAR_FIRST for other in (1, 0) if over or step or other]
+    for each in others:
+        layer_copy(*each).start()
+    for each in others:
+        layer_copy(*each).wait_send()
     cross.wait_send()
     for slot in range(SLOTS):
         for partner in range(3):
@@ -442,6 +453,12 @@
             else:
                 ring_copy(slot, way).wait_send()
             half_copy(slot, way).wait_send()
+    total = packed[layer, core]
+    for over, step, other in reversed(others):
+        layer_copy(over, step, other).wait_recv()
+        total += gathered[over * 4 + step, other]
+    out_ref[0:16, :] = total[:, :WIDTH]
+    out_ref[16:32, :] = total[:, WIDTH:]
 
 
 def shards(train_grads, query_pre, basis_in, basis_out):
@@ -482,7 +499,7 @@
             pltpu.VMEM((LAYERS, 2, 16, LANES), F32),
             dma((2,)), dma((MODULES,)), dma((SLOTS,)), dma((SLOTS,)),
             dma((SLOTS, 3)), dma((SLOTS, 3)), dma((2, 4, 2)), dma((2, 4, 2)), dma((SLOTS, 2)), dma((SLOTS, 2)), dma((SLOTS, 2)), dma((SLOTS, 2)),
-            dma((SLOTS, 3)), dma((SLOTS, 3)), dma, dma, dma((LAYERS, 2)), dma((LAYERS, 2)),
+            dma((SLOTS, 3)), dma((SLOTS, 3)), dma, dma, dma((LAYERS, 2)), dma((LAYERS, 2)), pltpu.SemaphoreType.REGULAR((3,)),
         ],
         compiler_params=pltpu.CompilerParams(
             collective_id=0, has_side_effects=True, vmem_limit_bytes=62 * 2**20

time: 135 us -> 135 us (level)
  no operation moved by 1% of the time
where the time goes in v5:
time: 135 us
  Pallas kernels  134 us (99%)
    pallas_call x1, Pallas kernels, shards(): pl.pallas_call(kernel, out_shape=jax.ShapeDtypeStruct((32, WIDTH), F32),...  134 us

profile of v5, /device:TPU:1, one launch (start us, length us, event | category | flops | bytes accessed | tf_op | source)
XLA Modules:
  0.0 135.1 jit_solution(29248790482465484)
XLA Ops:
  0.0 133.7 %influence_scores.1 = f32[32,64]{1,0:T(8,128)} custom-call(bf16[20,16,4096]{2,1,0:T(8,128)(2,1)} %bitcast.3, bf16[20,64,4096]{2,1,0:T(8,128)(2,1)} %bitcast.2, bf16[20,64,64]{2,1,0:T(8,128)(2,1)} %inner_hbm.1, bf16[20,64,64]{2,1,0:T(8,128)(2,1)} %outer_hbm.1), custom_call_target="tpu_custom_call" | custom-call | tf_op jit(solution)/shard_map/influence_scores/pallas_call | solution.py:466
  133.7 1.3 copy.6

commit v6 on v5

--- a/solution.py
+++ b/solution.py
@@ -19,7 +19,7 @@
 FIRST = 3
 LAST = 6
 EXTRA = 7
-SHARED = 1024
+SHARED = 896
 REST = FLAT - SHARED
 IN_PIECES = (FIRST, 0)
 FAR_FIRST = ((1, 2), (1, 1), (1, 3), (0, 2), (1, 0), (0, 1), (0, 3), (0, 0))
@@ -413,18 +413,6 @@
     wait_queries(LAST)
     for step in (0, 1, 3):
         score_part(step)
-    for way in range(2):
-        half_copy(LAST, way).wait_recv()
-    score_part(2)
-    cross.wait_recv()
-    own = pair_scores[0] + column_scores[...] + theirs[...]
-    moved = pltpu.roll(own, WIDTH, 1)
-    left = iota((LAYERS, 16, LANES), 2) < WIDTH
-    own = own.reshape(LAYERS, 2, 16, LANES)
-    moved = moved.reshape(LAYERS, 2, 16, LANES)
-    packed[:, 0] = jnp.where(left, own[:, 0], moved[:, 1])
-    packed[:, 1] = jnp.where(left, moved[:, 0], own[:, 1])
-
     def layer_copy(over, step, other):
         return pltpu.make_async_remote_copy(
             src_ref=packed.at[layer_at(over, step), 1 - core if other else core],
@@ -435,9 +423,36 @@
             device_id_type=MESH,
         )
 
+    def pack(first, count):
+        rows = pl.ds(pl.multiple_of(first * 32, 32), count * 32)
+        own = pair_scores[0, rows, :] + column_scores[rows, :] + theirs[rows, :]
+        moved = pltpu.roll(own, WIDTH, 1)
+        left = iota((count, 16, LANES), 2) < WIDTH
+        own = own.reshape(count, 2, 16, LANES)
+        moved = moved.reshape(count, 2, 16, LANES)
+        packed[pl.ds(first, count), 0] = jnp.where(left, own[:, 0], moved[:, 1])
+        packed[pl.ds(first, count), 1] = jnp.where(left, moved[:, 0], own[:, 1])
+
     others = [(over, step, other) for over, step in FAR_FIRST for other in (1, 0) if over or step or other]
-    for each in others:
-        layer_copy(*each).start()
+    opposite = (z + 2) % DEPTH
+
+    def start_sums(late):
+        for over, step in FAR_FIRST:
+
+            @pl.when((layer_at(over, step) // 2 == opposite) == late)
+            def _():
+                for other in (1, 0):
+                    if over or step or other:
+                        layer_copy(over, step, other).start()
+
+    cross.wait_recv()
+    pack(0, LAYERS)
+    start_sums(False)
+    for way in range(2):
+        half_copy(LAST, way).wait_recv()
+    score_part(2)
+    pack(2 * opposite, 2)
+    start_sums(True)
     for each in others:
         layer_copy(*each).wait_send()
     cross.wait_send()

time: 135 us -> 135 us (level)
  no operation moved by 1% of the time
where the time goes in v6:
time: 135 us
  Pallas kernels  133 us (99%)
    pallas_call x1, Pallas kernels, shards(): pl.pallas_call(kernel, out_shape=jax.ShapeDtypeStruct((32, WIDTH), F32),...  133 us

profile of v6, /device:TPU:1, one launch (start us, length us, event | category | flops | bytes accessed | tf_op | source)
XLA Modules:
  0.0 134.8 jit_solution(16271711303188388046)
XLA Ops:
  0.0 133.5 %influence_scores.1 = f32[32,64]{1,0:T(8,128)} custom-call(bf16[20,16,4096]{2,1,0:T(8,128)(2,1)} %bitcast.3, bf16[20,64,4096]{2,1,0:T(8,128)(2,1)} %bitcast.2, bf16[20,64,64]{2,1,0:T(8,128)(2,1)} %inner_hbm.1, bf16[20,64,64]{2,1,0:T(8,128)(2,1)} %outer_hbm.1), custom_call_target="tpu_custom_call" | custom-call | tf_op jit(solution)/shard_map/influence_scores/pallas_call | solution.py:481
  133.5 1.3 copy.6
